TPU v7x, 256 devices: a whole 4x4x8 slice. The times are simulated.
256 devices in a mesh: lat: 32 (over x, z_lo, core), lon: 8 (over z_hi, y).
Axes of the slice: x: 4, y: 4, z: 8 (z_hi: 2, z_lo: 4; z = z_hi * 4 + z_lo), core: 2. Of those that a mesh axis runs over, the one named last changes fastest.
Arguments:
- grid_input: bfloat16 [704, 1440, 256], P('lat', 'lon'), may hold values from -1.5 to 1.5
- cotangent: bfloat16 [704, 1440, 256], P('lat', 'lon'), may hold values from -6 to 6
- mixing: bfloat16 [384, 256, 256], P('lat', 'lon'), may hold values from -0.375 to 0.375
Outputs:
- input_grad: bfloat16 [704, 1440, 256], P('lat', 'lon')
- weight_grad: float32 [384, 256, 256], P('lat', 'lon')
All inputs are finite; a program needn't handle non-finite values.
Results may differ from a plain program's by a relative error of at most 0.0083.
Values may be sent and summed in bfloat16 or wider, within the bound.
No kernel may reach another device: no remote copies, remote signals or barrier semaphores. Data moves between devices by JAX's collectives and lax.ppermute only.
A program may use at most 128 MiB of HBM per device.

v0:
```python
import math

import jax
import jax.numpy as jnp
from jax import lax
from jax.experimental import pallas as pl
from jax.experimental.pallas import tpu as pltpu
from jax.sharding import Mesh, PartitionSpec as P

F32 = jnp.float32
BF16 = jnp.bfloat16
NLON, NLAT, ORDERS, DEGREES = 1440, 704, 384, 384
ROWS, POINTS, CH = 22, 180, 256
RING = ("zlo", "zhi", "y")
CROSS = ("x", "core")
NT = (((1,), (1,)), ((), ()))
TN = (((0,), (0,)), ((), ()))
SMEM = pl.BlockSpec(memory_space=pltpu.SMEM)
PIECE = jax.ShapeDtypeStruct((768, 128), BF16)


def call(body, outs, ins, grid=(1,), scratch=(), us=1, specs=None, out_specs=None, name=None):
    whole = lambda a: pl.BlockSpec(a.shape, lambda *_, n=len(a.shape): (0,) * n)
    specs = specs or [None] * len(ins)
    return pl.pallas_call(
        body,
        out_shape=outs,
        grid=grid,
        in_specs=[whole(a) if s is None else s for a, s in zip(ins, specs)],
        out_specs=out_specs or jax.tree.map(whole, outs),
        scratch_shapes=list(scratch),
        compiler_params=pltpu.CompilerParams(vmem_limit_bytes=56 * 2**20),
        cost_estimate=pl.CostEstimate(
            flops=us * 1_100_000_000, bytes_accessed=us * 1_000_000, transcendentals=0
        ),
        name=name,
    )(*ins)


def partner(position, k):
    dx, dc = divmod(k, 2)
    x, core = position // 2, position % 2
    core = (core + dc) % 2
    return ((x + dx) % 4) * 2 + core, ((x + 4 - dx) % 4) * 2 + core


def pack_kernel(p_ref, x_ref, o_ref, s_ref):
    south = p_ref[0] >= 4
    eye = (
        lax.broadcasted_iota(jnp.int32, (CH, CH), 0) == lax.broadcasted_iota(jnp.int32, (CH, CH), 1)
    ).astype(BF16)
    zeros = jnp.zeros((CH, 76), F32)
    for pair in range(11):
        tail = None
        for parity in range(2):
            j = 2 * pair + parity
            j = jnp.where(south, 21 - j, j)
            head = lax.dot_general(eye, x_ref[j, 0:128, :], NT, preferred_element_type=F32)
            row = (parity * 11 + pair) * 8
            s_ref[:, row : row + 8, :] = head.reshape(32, 8, 128)
            rest = lax.dot_general(eye, x_ref[j, 128:180, :], NT, preferred_element_type=F32)
            rest = jnp.concatenate([rest, zeros], axis=1)
            tail = rest if parity == 0 else tail + pltpu.roll(rest, 64, 1)
        row = 176 + pair * 8
        s_ref[:, row : row + 8, :] = tail.reshape(32, 8, 128)
    o_ref[...] = s_ref[...].astype(BF16)


def pack(position, x):
    return call(
        pack_kernel,
        jax.ShapeDtypeStruct((32, 264, 128), BF16),
        [position, x],
        scratch=[pltpu.VMEM((32, 264, 128), F32)],
        specs=[SMEM, None],
        us=5,
        name="pack",
    )


def waves_kernel(c_ref, s_ref, f_ref, b_ref):
    for d in range(8):
        rows = slice(d * 96, d * 96 + 96)
        order = 8 * (lax.broadcasted_iota(jnp.int32, (96, 128), 0) // 2) + d
        factor = jnp.where(order == 0, 1.0 / NLON, 2.0 / NLON)
        low = lax.broadcasted_iota(jnp.int32, (96, 128), 1) < 64

        def turned(o, lanes):
            angle = (d * o) % 8 * math.pi / 4
            return c_ref[rows, lanes] * math.cos(angle) - s_ref[rows, lanes] * math.sin(angle)

        def put(value, place):
            f_ref[rows, place * 128 : place * 128 + 128] = value.astype(BF16)
            b_ref[rows, place * 128 : place * 128 + 128] = (value * factor).astype(BF16)

        for o in range(8):
            put(turned(o, slice(0, 128)), o)
        for o in range(4):
            tails = [turned(2 * o + i, slice(128, 256)) for i in range(2)]
            put(jnp.where(low, tails[0], tails[1]), 8 + o)


def fourier_tables():
    q = jnp.arange(768, dtype=jnp.int32)
    order, quarter = 8 * (q % 96 // 2) + q // 96, q % 2
    lane = jnp.arange(256, dtype=jnp.int32)
    point = jnp.where(lane < 128, lane, 128 + lane % 64)
    valid = (point < POINTS)[None, :]
    phase = (point[None, :] * order[:, None] + 360 * quarter[:, None]) % NLON
    angle = phase.astype(F32) * (2.0 * math.pi / NLON)
    table = jax.ShapeDtypeStruct((768, 1536), BF16)
    return call(
        waves_kernel,
        (table, table),
        [jnp.where(valid, jnp.cos(angle), 0.0), jnp.where(valid, jnp.sin(angle), 0.0)],
        us=4,
        name="waves",
    )


def fourier_kernel(p_ref, r_ref, f_ref, w_ref, *refs):
    o_refs, (s_ref, k_ref, t_ref) = refs[:8], refs[8:]
    position = p_ref[0]
    south = position >= 4
    s_ref[0 : 32 * 264, :] = r_ref[...].reshape(32 * 264, 128).astype(F32)
    s_ref[32 * 264 :, :] = jnp.zeros((64, 128), F32)
    low = lax.broadcasted_iota(jnp.int32, (16, 128), 1) < 64

    def one(pair, _):
        for b in range(2):
            c = 2 * pair + b
            for zlo in range(4):
                source = jnp.where(south, 3 - zlo, zlo) * (8 * 264) + c
                row = b * 128 + zlo * 32
                tails = []
                for o in range(8):
                    base = source + o * 264
                    for parity in range(2):
                        k_ref[row + parity * 16 : row + parity * 16 + 16, o * 128 : o * 128 + 128] = (
                            s_ref[pl.ds(base + parity * 88, 16, stride=8), :].astype(BF16)
                        )
                    tails.append(s_ref[pl.ds(base + 176, 16, stride=8), :])
                for o in range(4):
                    even, odd = tails[2 * o], tails[2 * o + 1]
                    lanes = slice(1024 + o * 128, 1152 + o * 128)
                    north = jnp.where(low, even, pltpu.roll(odd, 64, 1))
                    k_ref[row : row + 16, lanes] = north.astype(BF16)
                    other = jnp.where(low, pltpu.roll(even, 64, 1), odd)
                    k_ref[row + 16 : row + 32, lanes] = other.astype(BF16)
        spec = lax.dot_general(f_ref[...], k_ref[...], NT, preferred_element_type=F32)
        for b in range(2):
            value = spec[:, b * 128 : b * 128 + 128] * w_ref[0:1, :]
            t_ref[pl.ds(2 * pair + b, 768, stride=8), :] = value
        return 0

    lax.fori_loop(0, 4, one, 0)
    for k in range(8):
        start = pl.multiple_of(partner(position, k)[0] * 768, 768)
        o_refs[k][...] = t_ref[pl.ds(start, 768), :].astype(BF16)


def fourier(position, received, table, weights):
    return call(
        fourier_kernel,
        (PIECE,) * 8,
        [position, received, table, weights],
        scratch=[
            pltpu.VMEM((32 * 264 + 64, 128), F32),
            pltpu.VMEM((256, 1536), BF16),
            pltpu.VMEM((6144, 128), F32),
        ],
        specs=[SMEM, None, None, None],
        us=9,
        name="fourier",
    )


def block_orders(i):
    return jnp.where(i < 6, i // 3, jnp.where(i < 10, 2 + (i - 6) // 2, i - 6))


def block_degrees(i):
    return jnp.where(i < 6, i % 3, jnp.where(i < 10, 1 + i % 2, 2))


def table_kernel(m_ref, cos_ref, log_ref, o_ref, s_ref, v_ref):
    i = pl.program_id(0)
    group, part = block_orders(i), block_degrees(i)

    @pl.when(part == group // 2)
    def _():
        v_ref[0] = jnp.zeros((8, 512), F32)
        v_ref[1] = jnp.zeros((8, 512), F32)
        v_ref[2] = log_ref[...]

    order = m_ref[...]
    square = order * order
    cosine = cos_ref[...]
    wide = lambda a: jnp.concatenate([a] * 4, axis=1)

    def steps(n, carried):
        previous, earlier, scale = carried
        size = jnp.exp(scale)
        for u in range(8):
            l = n * 8 + u
            degree = jnp.full((8, 128), part * 128 + l, jnp.int32).astype(F32)
            below = (degree - 1.0) * (degree - 1.0)
            growth = jnp.sqrt(
                jnp.maximum(4.0 * degree * degree - 1.0, 0.0)
                / jnp.maximum(degree * degree - square, 1.0)
            )
            shrink = jnp.sqrt(
                jnp.maximum(below - square, 0.0) / jnp.maximum(4.0 * below - 1.0, 1.0)
            )
            current = wide(growth) * (cosine * previous) - wide(growth * shrink) * earlier
            current = jnp.where(wide(degree == order), 1.0, current)
            value = current * size
            for d in range(4):
                s_ref[d, pl.ds(pl.multiple_of(l * 8, 8), 8), :] = value[:, d * 128 : d * 128 + 128]
            previous, earlier = current, previous
        over = jnp.maximum(jnp.abs(previous), jnp.abs(earlier)) > 1e5
        factor = jnp.where(over, 1e-10, 1.0)
        scale = scale + jnp.where(over, math.log(1e10), 0.0)
        return previous * factor, earlier * factor, scale

    state = lax.fori_loop(0, 16, steps, (v_ref[0], v_ref[1], v_ref[2]))
    for n in range(3):
        v_ref[n] = state[n]
    for s in range(8):
        for d in range(4):
            o_ref[0, s, :, d * 128 : d * 128 + 128] = s_ref[
                d, pl.ds(s, 128, stride=8), :
            ].astype(BF16)


def legendre_table(orders, cosine, logs):
    return call(
        table_kernel,
        jax.ShapeDtypeStruct((12, 8, 128, 512), BF16),
        [orders, cosine, logs],
        grid=(12,),
        scratch=[pltpu.VMEM((4, 1024, 128), F32), pltpu.VMEM((3, 8, 512), F32)],
        specs=[
            pl.BlockSpec((8, 128), lambda i: (block_orders(i), 0)),
            None,
            pl.BlockSpec((8, 512), lambda i: (block_orders(i), 0)),
        ],
        out_specs=pl.BlockSpec((1, 8, 128, 512), lambda i: (i, 0, 0, 0)),
        us=25,
        name="legendre",
    )


def pick(g, *values):
    out = values[-1]
    for n in reversed(range(len(values) - 1)):
        out = jnp.where(g == n, values[n], out)
    return out


TABLE = [
    pl.BlockSpec((1, 8, 128, 512), lambda g, v=v: (pick(g, *v), 0, 0, 0))
    for v in ((0, 3), (1, 4, 6, 8), (2, 5, 7, 9, 10, 11))
]


def by_parts(group, body):
    for first in range(3):

        @pl.when(group // 2 == first)
        def _(first=first):
            body(first)


def signs(position, rows):
    lane = lax.broadcasted_iota(jnp.int32, (rows, 128), 1)
    return jnp.where((lane + position) % 2 == 0, 1.0, -1.0)


def analyse_kernel(p_ref, *refs):
    pieces, t_refs, (o_ref, s_ref, c_ref, q_ref) = refs[:8], refs[8:11], refs[11:]
    group = pl.program_id(0)
    position = p_ref[0]

    @pl.when(group == 0)
    def _():
        for k in range(8):
            s_ref[partner(position, k)[1]] = pieces[k][...]
        c_ref[...] = jnp.zeros_like(c_ref)

    sign = signs(position, 16)

    def body(first):
        for s in range(8):
            row = pl.multiple_of(group * 128 + s * 16, 16)
            north = jnp.concatenate([s_ref[d, pl.ds(row, 16), :] for d in range(4)], axis=1)
            south = jnp.concatenate([s_ref[7 - d, pl.ds(row, 16), :] for d in range(4)], axis=1)
            value = lax.dot_general(
                jnp.concatenate([north, south], axis=0),
                jnp.concatenate([t_refs[b][0, s] for b in range(first, 3)], axis=0),
                NT,
                preferred_element_type=F32,
            )
            for b in range(first, 3):
                lanes = slice((b - first) * 128, (b - first) * 128 + 128)
                c_ref[b, pl.ds(row, 16), :] = value[0:16, lanes] + sign * value[16:32, lanes]

    by_parts(group, body)

    @pl.when(group == 5)
    def _():
        lane = lax.broadcasted_iota(jnp.int32, (96, 128), 1)
        for c in range(8):
            block = jnp.concatenate(
                [c_ref[b, pl.ds(c, 96, stride=8), :] for b in range(3)], axis=1
            )
            block = jnp.concatenate([block, jnp.zeros((32, DEGREES), F32)], axis=0).T
            first = jnp.where(lane < 96, block[288:384], pltpu.roll(block[0:96], 96, 1))
            second = jnp.where(lane < 72, block[192:288], pltpu.roll(block[96:192], 72, 1))
            q_ref[0, pl.ds(c, 96, stride=8), :] = first
            q_ref[1, pl.ds(c, 96, stride=8), :] = second
        o_ref[...] = jnp.concatenate(
            [q_ref[0].reshape(32, 24, 128), q_ref[1].reshape(32, 24, 128)], axis=1
        ).astype(BF16)


def analyse(position, pieces, table):
    return call(
        analyse_kernel,
        jax.ShapeDtypeStruct((32, 48, 128), BF16),
        [position, *pieces, table, table, table],
        grid=(6,),
        scratch=[
            pltpu.VMEM((8, 768, 128), BF16),
            pltpu.VMEM((3, 768, 128), F32),
            pltpu.VMEM((2, 768, 128), F32),
        ],
        specs=[SMEM] + [None] * 8 + TABLE,
        us=10,
        name="analyse",
    )


def pair_rows(ref, p):
    return ref[:, p * 8 : p * 8 + 8, :].astype(F32).reshape(CH, 128).astype(BF16)


def mix_kernel(a_ref, w_ref, o_ref):
    lane = lax.broadcasted_iota(jnp.int32, (CH, 128), 1)
    pieces = []
    for p in range(6):
        half, e = divmod(p, 3)
        rows = pair_rows(a_ref, p)
        high = jnp.dot(w_ref[3 - half, :, e].reshape(CH, CH), rows, preferred_element_type=F32)
        low = jnp.dot(w_ref[half, :, e].reshape(CH, CH), rows, preferred_element_type=F32)
        pieces.append(jnp.where(lane < 96 - 24 * half, high, low).reshape(32, 8, 128))
    o_ref[...] = jnp.concatenate(pieces, axis=1).astype(BF16)


def mix(adjoint, mixing):
    return call(
        mix_kernel,
        jax.ShapeDtypeStruct((32, 48, 128), BF16),
        [adjoint, mixing],
        us=3,
        name="mix",
    )


PARTS = jax.ShapeDtypeStruct((4, 3, 128, CH), F32)


def grad_kernel(p_ref, c_ref, a_ref, near_ref, far_ref, s_ref):
    lane = lax.broadcasted_iota(jnp.int32, (CH, 128), 1)
    for p in range(6):
        half, e = divmod(p, 3)
        left, right = pair_rows(c_ref, p), pair_rows(a_ref, p)
        inside = lane < 96 - 24 * half
        zero = jnp.zeros_like(left)
        high = lax.dot_general(jnp.where(inside, left, zero), right, NT, preferred_element_type=F32)
        low = lax.dot_general(jnp.where(inside, zero, left), right, NT, preferred_element_type=F32)
        for n in range(2):
            s_ref[2 * (3 - half) + n, e] = high[n * 128 : n * 128 + 128]
            s_ref[2 * half + n, e] = low[n * 128 : n * 128 + 128]
    for dx in range(4):
        near_ref[dx] = s_ref[partner(p_ref[0], 2 * dx)[0]]
        far_ref[dx] = s_ref[partner(p_ref[0], 2 * dx + 1)[0]]


def weight_sums(position, coefficients, adjoint):
    return call(
        grad_kernel,
        (PARTS, PARTS),
        [position, coefficients, adjoint],
        scratch=[pltpu.VMEM((8, 3, 128, CH), F32)],
        specs=[SMEM, None, None],
        us=4,
        name="grad",
    )


def add_kernel(a_ref, b_ref, *o_refs):
    for dx in range(4):
        o_refs[dx][...] = a_ref[dx] + b_ref[dx]


def add_cores(near, far):
    piece = jax.ShapeDtypeStruct((3, 128, CH), F32)
    return call(add_kernel, (piece,) * 4, [near, far], us=3, name="add")


def total_kernel(y_ref, *refs):
    pieces, o_refs, s_ref = refs[:4], refs[4:8], refs[8]
    s_ref[...] = (pieces[0][...] + pieces[1][...]) + (pieces[2][...] + pieces[3][...])
    for step in range(4):
        row = pl.multiple_of((y_ref[0] + step) % 4 * 32, 32)
        o_refs[step][...] = s_ref[:, pl.ds(row, 32), :]


def total_sums(y, pieces):
    return call(
        total_kernel,
        (jax.ShapeDtypeStruct((3, 32, CH), F32),) * 4,
        [y, *pieces],
        scratch=[pltpu.VMEM((3, 128, CH), F32)],
        specs=[SMEM] + [None] * 4,
        us=3,
        name="total",
    )


def gather_kernel(p_ref, *refs):
    for k in range(8):
        refs[8][partner(p_ref[0], k)[1]] = refs[k][...]


def gather(position, pieces):
    return call(
        gather_kernel,
        jax.ShapeDtypeStruct((8, 3, 128, CH), BF16),
        [position, *pieces],
        specs=[SMEM] + [None] * 8,
        us=2,
        name="gather",
    )


def synthesise_kernel(p_ref, m_ref, w_ref, *refs):
    t_refs, o_refs, (q_ref, c_ref, b_ref) = refs[:3], refs[3:11], refs[11:]
    group = pl.program_id(0)
    position = p_ref[0]

    @pl.when(group == 0)
    def _():
        mixed = m_ref[...].astype(F32)
        q_ref[0] = mixed[:, 0:24, :].reshape(768, 128)
        q_ref[1] = mixed[:, 24:48, :].reshape(768, 128)
        for c in range(8):
            first = q_ref[0, pl.ds(c, 96, stride=8), :]
            second = q_ref[1, pl.ds(c, 96, stride=8), :]
            block = jnp.concatenate(
                [pltpu.roll(first, 32, 1), pltpu.roll(second, 56, 1), second, first], axis=0
            )
            block = block.T[0:96, :]
            for b in range(3):
                c_ref[b, pl.ds(c, 96, stride=8), :] = block[:, b * 128 : b * 128 + 128]

    sign = signs(position, 16)

    def body(first):
        for s in range(8):
            row = pl.multiple_of(group * 128 + s * 16, 16)
            north = [c_ref[b, pl.ds(row, 16), :] for b in range(first, 3)]
            south = [a * sign for a in north]
            left = jnp.concatenate(
                [jnp.concatenate(north, axis=1), jnp.concatenate(south, axis=1)], axis=0
            ).astype(BF16)
            right = jnp.concatenate([t_refs[b][0, s] for b in range(first, 3)], axis=0)
            value = jnp.dot(left, right, preferred_element_type=F32)
            for d in range(4):
                lanes = slice(d * 128, d * 128 + 128)
                mirror = slice((7 - d) * 128, (7 - d) * 128 + 128)
                b_ref[d, pl.ds(row, 16), :] = (value[0:16, lanes] * w_ref[0:1, lanes]).astype(BF16)
                b_ref[7 - d, pl.ds(row, 16), :] = (
                    value[16:32, lanes] * w_ref[0:1, mirror]
                ).astype(BF16)

    by_parts(group, body)

    @pl.when(group == 5)
    def _():
        for k in range(8):
            o_refs[k][...] = b_ref[partner(position, k)[0]]


def synthesise(position, mixed, table, weights):
    return call(
        synthesise_kernel,
        (PIECE,) * 8,
        [position, mixed, weights, table, table, table],
        grid=(6,),
        scratch=[
            pltpu.VMEM((2, 768, 128), F32),
            pltpu.VMEM((3, 768, 128), F32),
            pltpu.VMEM((8, 768, 128), BF16),
        ],
        specs=[SMEM, None, None] + TABLE,
        us=10,
        name="synthesise",
    )


def inverse_kernel(p_ref, *refs):
    pieces, (f_ref, o_ref, s_ref, t_ref) = refs[:8], refs[8:]
    position = p_ref[0]
    south = position >= 4
    for k in range(8):
        start = pl.multiple_of(partner(position, k)[1] * 768, 768)
        s_ref[pl.ds(start, 768), :] = pieces[k][...].astype(F32)
    low = lax.broadcasted_iota(jnp.int32, (11, 128), 1) < 64

    def one(pair, _):
        left = jnp.concatenate(
            [s_ref[pl.ds(2 * pair + b, 768, stride=8), :].astype(BF16) for b in range(2)], axis=1
        )
        grid = lax.dot_general(left, f_ref[...], TN, preferred_element_type=F32)
        for b in range(2):
            for zlo in range(4):
                place = jnp.where(south, 3 - zlo, zlo) * (8 * 264) + 2 * pair + b
                row = b * 128 + zlo * 32
                even, odd = grid[row : row + 11], grid[row + 16 : row + 27]
                for o in range(8):
                    base = place + o * 264
                    lanes = slice(o * 128, o * 128 + 128)
                    t_ref[pl.ds(base, 11, stride=8), :] = even[:, lanes]
                    t_ref[pl.ds(base + 88, 11, stride=8), :] = odd[:, lanes]
                    lanes = slice(1024 + o // 2 * 128, 1152 + o // 2 * 128)
                    first, last = even[:, lanes], odd[:, lanes]
                    if o % 2 == 0:
                        tail = jnp.where(low, first, pltpu.roll(last, 64, 1))
                    else:
                        tail = jnp.where(low, pltpu.roll(first, 64, 1), last)
                    t_ref[pl.ds(base + 176, 11, stride=8), :] = tail
        return 0

    lax.fori_loop(0, 4, one, 0)
    o_ref[...] = t_ref[...].reshape(32, 264, 128).astype(BF16)


def inverse(position, pieces, table):
    return call(
        inverse_kernel,
        jax.ShapeDtypeStruct((32, 264, 128), BF16),
        [position, *pieces, table],
        scratch=[pltpu.VMEM((6144, 128), F32), pltpu.VMEM((32 * 264, 128), F32)],
        specs=[SMEM] + [None] * 9,
        us=9,
        name="inverse",
    )


def finish_kernel(p_ref, r_ref, g_ref, o_ref, s_ref):
    south = p_ref[0] >= 4
    s_ref[...] = r_ref[...].astype(F32)
    for pair in range(11):
        row = 176 + pair * 8
        tail = s_ref[:, row : row + 8, :].reshape(CH, 128).T
        for parity in range(2):
            j = 2 * pair + parity
            j = jnp.where(south, 21 - j, j)
            row = (parity * 11 + pair) * 8
            head = s_ref[:, row : row + 8, :].reshape(CH, 128).T
            o_ref[j, 0:128, :] = (g_ref[j, 0:128, :].astype(F32) + head).astype(BF16)
            rest = tail[parity * 64 : parity * 64 + 52]
            o_ref[j, 128:180, :] = (g_ref[j, 128:180, :].astype(F32) + rest).astype(BF16)


def finish(position, received, cotangent):
    return call(
        finish_kernel,
        jax.ShapeDtypeStruct((ROWS, POINTS, CH), BF16),
        [position, received, cotangent],
        scratch=[pltpu.VMEM((32, 264, 128), F32)],
        specs=[SMEM, None, None],
        us=4,
        name="finish",
    )


def swap(value):
    return lax.all_to_all(value, RING, split_axis=0, concat_axis=0, tiled=True)


def cross(pieces):
    moved = [pieces[0]]
    for k in range(1, 8):
        pairs = [(p, partner(p, k)[0]) for p in range(8)]
        moved.append(lax.ppermute(pieces[k], CROSS, pairs))
    return moved


def along_x(pieces):
    return [pieces[0]] + [
        lax.ppermute(pieces[dx], "x", [(i, (i + dx) % 4) for i in range(4)]) for dx in range(1, 4)
    ]


def other_core(value):
    return lax.ppermute(value, "core", [(0, 1), (1, 0)])


def turned(pieces):
    moved = []
    for step, piece in enumerate(pieces):
        pairs = [
            (core * 8 + zhi * 4 + y, zhi * 8 + core * 4 + (y + step) % 4)
            for core in range(2)
            for zhi in range(2)
            for y in range(4)
        ]
        moved.append(lax.ppermute(piece, ("core", "zhi", "y"), pairs))
    return moved


def in_order(pieces):
    y = lax.axis_index("y")
    out = jnp.zeros((4, *pieces[0].shape), pieces[0].dtype)
    for step, piece in enumerate(pieces):
        out = lax.dynamic_update_index_in_dim(out, piece, (y + 4 - step) % 4, 0)
    return out


def after(value, *others):
    return lax.optimization_barrier((value, *others))[0]


def slot_rows():
    slot = jnp.arange(512, dtype=jnp.int32)
    device, within = slot // 128, slot % 128
    zlo, parity, pair = within // 32, within % 32 // 16, within % 16
    row = (device // 2) * 176 + zlo * 44 + (device % 2) * 22 + 2 * pair + parity
    mirrored = (NLAT - 1 - row).reshape(4, 128)[::-1].reshape(512)
    valid = pair < 11
    return jnp.concatenate([row, mirrored]), jnp.concatenate([valid, valid])


def local(grid_input, cotangent, mixing):
    position = lax.axis_index("x") * 2 + lax.axis_index("core")
    y = lax.axis_index("y")
    where = jnp.full((1,), position, jnp.int32)
    packed_g = pack(where, cotangent)
    sent_g = swap(packed_g)
    packed_x = pack(where, after(grid_input, packed_g))
    mixing = after(mixing, packed_g)
    weights = in_order(
        turned([lax.dynamic_slice_in_dim(mixing, (y + step) % 4 * 3, 3, 0) for step in range(4)])
    )
    weights = jnp.transpose(weights, (1, 0, 2, 3)).reshape(3, 128, CH)
    row, valid = slot_rows()
    colatitude = (row.astype(F32) + 0.5) * (math.pi / NLAT)
    sine = jnp.sin(colatitude)
    quadrature = jnp.where(valid, math.pi / NLAT * sine, 0.0)
    cosine = jnp.where(valid, jnp.cos(colatitude), 0.0)[0:512]
    orders = 8 * jnp.arange(48, dtype=jnp.int32) + position
    order_value = orders.astype(F32)[:, None]
    counter = jnp.arange(1, ORDERS + 1, dtype=F32)[None, :]
    log_terms = jnp.where(counter <= order_value, jnp.log1p(0.5 / counter), 0.0)
    logs = (
        0.5 * math.log(0.5)
        + 0.5 * jnp.sum(log_terms, axis=1, keepdims=True)
        + order_value * jnp.log(sine[0:512])[None, :]
    )
    logs = jnp.where(valid[None, 0:512], logs, -1e30)
    table = legendre_table(
        after(jnp.broadcast_to(order_value, (48, 128)), packed_x),
        jnp.broadcast_to(cosine[None, :], (8, 512)),
        logs,
    )
    forward, backward = fourier_tables()
    own = lax.dynamic_slice_in_dim(quadrature, position * 128, 128)
    sent_g = after(sent_g, packed_x, forward, backward, table, weights)
    sent_x = swap(after(packed_x, sent_g))
    pieces_g = fourier(where, sent_g, backward, jnp.ones((8, 128), F32))
    packed_adjoint = analyse(where, cross(pieces_g), table)
    adjoint = swap(after(packed_adjoint, sent_x))
    weights = along_x([after(weights, packed_adjoint, sent_x)] * 4)
    weights = [w for near in weights for w in (near, other_core(near))]
    weights = gather(where, weights).reshape(4, 2, 3, 128, CH)
    pieces_x = fourier(where, sent_x, forward, jnp.broadcast_to(own[None, :], (8, 128)))
    mixed = swap(mix(after(adjoint, pieces_x[0]), weights))
    coefficients = analyse(where, cross(pieces_x), table)
    mixed = after(mixed, coefficients)
    back = synthesise(where, mixed, table, jnp.broadcast_to(quadrature[None, :], (8, 1024)))
    coefficients = swap(after(coefficients, back[0]))
    packed_back = inverse(where, cross(back), forward)
    grid_back = swap(packed_back)
    near, far = weight_sums(where, after(coefficients, packed_back), adjoint)
    total = along_x(add_cores(near, other_core(far)))
    total = turned(total_sums(jnp.full((1,), y, jnp.int32), total))
    input_grad = finish(where, grid_back, cotangent)
    total[0] = after(total[0], input_grad)
    return input_grad, in_order(total).reshape(12, 32, CH)


def solution(mesh):
    fine = Mesh(mesh.devices.reshape(4, 4, 2, 2, 4), ("x", "zlo", "core", "zhi", "y"))
    spec = P(("x", "zlo", "core"), ("zhi", "y"), None)
    return jax.shard_map(
        local, mesh=fine, in_specs=(spec, spec, spec), out_specs=(spec, spec), check_vma=False
    )
```

profile of v0, /device:TPU:1, one launch (start us, length us, event | category | flops | bytes accessed | tf_op | source)
XLA Modules:
  0.0 315.4 jit_solution(8086587914577374046)
XLA Ops:
  0.6 4.7 %pack.2 = bf16[32,264,128]{2,1,0:T(8,128)(2,1)} custom-call(s32[1]{0:T(128)} %bitcast.p_ref, bf16[22,180,256]{2,1,0:T(8,128)(2,1)} %g_ref.1), custom_call_target="tpu_custom_call" | custom-call | flops 5500000256 | bytes 5000000 | tf_op jit(solution)/shard_map/pack/pallas_call | solution.py:25
  5.3 12.2 %all-to-all-start = ((bf16[32,264,128]{2,1,0:T(8,128)(2,1)}), bf16[32,264,128]{2,1,0:T(8,128)(2,1)S(1)}, u32[]{:S(2)}, u32[]{:S(2)}) async-start(bf16[32,264,128]{2,1,0:T(8,128)(2,1)} %pack.2), calls=%async_computation | async-start | bytes 4325376 | tf_op jit(solution)/shard_map/all_to_all | solution.py:591
  17.6 8.4 %collective-permute-start.3 = (bf16[3,32,256]{2,1,0:T(8,128)(2,1)S(1)}, bf16[3,32,256]{2,1,0:T(8,128)(2,1)S(1)}, u32[]{:S(2)}, u32[]{:S(2)}) collective-permute-start(bf16[3,32,256]{2,1,0:T(8,128)(2,1)S(1)} %get-tuple-element.98), channel_id=1, source_target_pairs={{0,3},{1,0},{2,1},{3,2},{4,11},{5,8},{6,9},{7,10},{8,7},{9,4},{10,... | collective-permute-start | bytes 147464 | tf_op jit(solution)/shard_map/ppermute | solution.py:621
  26.4 5.8 %collective-permute-start.1 = (bf16[3,32,256]{2,1,0:T(8,128)(2,1)S(1)}, bf16[3,32,256]{2,1,0:T(8,128)(2,1)S(1)}, u32[]{:S(2)}, u32[]{:S(2)}) collective-permute-start(bf16[3,32,256]{2,1,0:T(8,128)(2,1)S(1)} %get-tuple-element.100), channel_id=1, source_target_pairs={{0,1},{1,2},{2,3},{3,0},{4,9},{5,10},{6,11},{7,8},{8,5},{9,6},{10,... | collective-permute-start | bytes 147464 | tf_op jit(solution)/shard_map/ppermute | solution.py:621
  34.6 4.6 %pack.3 = bf16[32,264,128]{2,1,0:T(8,128)(2,1)} custom-call(s32[1]{0:T(128)} %bitcast.p_ref, bf16[22,180,256]{2,1,0:T(8,128)(2,1)} %x_ref.2), custom_call_target="tpu_custom_call" | custom-call | flops 5500000256 | bytes 5000000 | tf_op jit(solution)/shard_map/pack/pallas_call | solution.py:25
  40.7 4.9 %sine_select_fusion = (f32[768,256]{1,0:T(8,128)}, f32[768,256]{1,0:T(8,128)}) fusion(s32[768]{0:T(1024)S(1)} %get-tuple-element.108, s32[768]{0:T(1024)S(1)} %get-tuple-element.107, s32[256]{0:T(256)S(1)} %compare_select_fusion, pred[256]{0:T(512)(128)(4,1)S(1)} %broadcast_compare_fusion.1), kind=kLoop, calls=%fused_computation.3 | loop fusion | flops 2359296 | bytes 1580288 | tf_op jit(solution)/shard_map/jit(_where)/select_n | solution.py:115
  46.2 23.9 %legendre.1.refs_8_.refs_9_.refs_10_.refs_0_.refs_1_.refs_2_ = bf16[12,8,128,512]{3,2,1,0:T(8,128)(2,1)} custom-call(f32[48,128]{1,0:T(8,128)} %broadcast_in_dim.123.m_ref, f32[8,512]{1,0:T(8,128)} %broadcast_in_dim.125.cos_ref, f32[48,512]{1,0:T(8,128)} %add_select_fusion.1.log_ref), custom_call_target="tpu_custom_call" | custom-call | flops 27499999232 | bytes 25000000 | tf_op jit(solution)/shard_map/legendre/pallas_call | solution.py:25
  70.1 4.5 %waves.1 = (bf16[768,1536]{1,0:T(8,128)(2,1)}, bf16[768,1536]{1,0:T(8,128)(2,1)}) custom-call(f32[768,256]{1,0:T(8,128)} %get-tuple-element.103.c_ref, f32[768,256]{1,0:T(8,128)} %get-tuple-element.102.s_ref), custom_call_target="tpu_custom_call" | custom-call | flops 4400000000 | bytes 4000000 | tf_op jit(solution)/shard_map/waves/pallas_call | solution.py:25
  76.2 6.1 %all-to-all-start.1 = ((bf16[32,264,128]{2,1,0:T(8,128)(2,1)}), bf16[32,264,128]{2,1,0:T(8,128)(2,1)}, u32[]{:S(2)}, u32[]{:S(2)}) async-start(bf16[32,264,128]{2,1,0:T(8,128)(2,1)} %pack.3), calls=%async_computation.1 | async-start | bytes 4325376 | tf_op jit(solution)/shard_map/all_to_all | solution.py:591
  82.8 8.1 %fourier.2 = (bf16[768,128]{1,0:T(8,128)(2,1)}, bf16[768,128]{1,0:T(8,128)(2,1)}, bf16[768,128]{1,0:T(8,128)(2,1)}, bf16[768,128]{1,0:T(8,128)(2,1)}, bf16[768,1...) custom-call(s32[1]{0:T(128)} %bitcast.p_ref, ...), custom_call_target="tpu_custom_call" | custom-call | flops 9900000256 | bytes 9000000 | tf_op jit(solution)/shard_map/fourier/pallas_call | solution.py:25
  90.9 3.6 %collective-permute-start.4 = (bf16[768,128]{1,0:T(8,128)(2,1)}, bf16[768,128]{1,0:T(8,128)(2,1)S(1)}, u32[]{:S(2)}, u32[]{:S(2)}) collective-permute-start(bf16[768,128]{1,0:T(8,128)(2,1)} %get-tuple-element.57), channel_id=1, source_target_pairs={{0,8},{8,0},{64,72},{72,64},{128,136},{136,128},{192,200},{200,192... | collective-permute-start | bytes 589832 | tf_op jit(solution)/shard_map/ppermute | solution.py:598
  107.4 4.8 %collective-permute-done.7.refs_4_ = bf16[768,128]{1,0:T(8,128)(2,1)S(1)} collective-permute-done((bf16[768,128]{1,0:T(8,128)(2,1)}, bf16[768,128]{1,0:T(8,128)(2,1)S(1)}, u32[]{:S(2)}, u32[]{:S(2)}) %collective-permute-start.7) | collective-permute-done | bytes 196640 | tf_op jit(solution)/shard_map/ppermute | solution.py:598
  112.1 4.6 %collective-permute-done.8.refs_5_ = bf16[768,128]{1,0:T(8,128)(2,1)S(1)} collective-permute-done((bf16[768,128]{1,0:T(8,128)(2,1)}, bf16[768,128]{1,0:T(8,128)(2,1)S(1)}, u32[]{:S(2)}, u32[]{:S(2)}) %collective-permute-start.8) | collective-permute-done | bytes 196640 | tf_op jit(solution)/shard_map/ppermute | solution.py:598
  118.5 10.5 %analyse.2 = bf16[32,48,128]{2,1,0:T(8,128)(2,1)} custom-call(s32[1]{0:T(128)} %bitcast.p_ref, bf16[768,128]{1,0:T(8,128)(2,1)} %get-tuple-element.56.refs_0_, bf16[768,128]{1,0:T(8,128)(2,1)} %copy-done.27, bf16[768,128]{1,0:T(8,128)(2,1)} %copy-done.30, bf16[768,128]{1,0:T(8,128)(2,1)} %copy-done.32, bf16[768,128]{1,0:T(8,128)(2,1)} %copy-done.34, ...), custom_call_target="tpu_custom_call" | custom-call | flops 11000000512 | bytes 10000000 | tf_op jit(solution)/shard_map/analyse/pallas_call | solution.py:25
  134.7 3.3 %collective-permute-start.11 = (bf16[3,128,256]{2,1,0:T(8,128)(2,1)S(1)}, bf16[3,128,256]{2,1,0:T(8,128)(2,1)S(1)}, u32[]{:S(2)}, u32[]{:S(2)}) collective-permute-start(bf16[3,128,256]{2,1,0:T(8,128)(2,1)S(1)} %bitcast.37), channel_id=1, source_target_pairs={{0,8},{8,0},{1,9},{9,1},{2,10},{10,2},{3,11},{11,3},{4,12},{12,4},... | collective-permute-start | bytes 589832 | tf_op jit(solution)/shard_map/ppermute | solution.py:609
  138.0 7.0 %all-to-all-start.2 = ((bf16[32,48,128]{2,1,0:T(8,128)(2,1)}), bf16[32,48,128]{2,1,0:T(8,128)(2,1)S(1)}, u32[]{:S(2)}, u32[]{:S(2)}) async-start(bf16[32,48,128]{2,1,0:T(8,128)(2,1)} %analyse.2), calls=%async_computation.2 | async-start | bytes 786432 | tf_op jit(solution)/shard_map/all_to_all | solution.py:591
  147.2 8.1 %fourier.3 = (bf16[768,128]{1,0:T(8,128)(2,1)}, bf16[768,128]{1,0:T(8,128)(2,1)}, bf16[768,128]{1,0:T(8,128)(2,1)}, bf16[768,128]{1,0:T(8,128)(2,1)}, bf16[768,1...) custom-call(s32[1]{0:T(128)} %bitcast.p_ref, ...), custom_call_target="tpu_custom_call" | custom-call | flops 9900000256 | bytes 9000000 | tf_op jit(solution)/shard_map/fourier/pallas_call | solution.py:25
  155.4 9.9 %collective-permute-start.19 = (bf16[768,128]{1,0:T(8,128)(2,1)}, bf16[768,128]{1,0:T(8,128)(2,1)S(1)}, u32[]{:S(2)}, u32[]{:S(2)}) collective-permute-start(bf16[768,128]{1,0:T(8,128)(2,1)} %get-tuple-element.70), channel_id=1, source_target_pairs={{0,64},{8,72},{64,128},{72,136},{128,192},{136,200},{192,0},{200,8... | collective-permute-start | bytes 589832 | tf_op jit(solution)/shard_map/ppermute | solution.py:598
  178.3 8.9 %all-to-all-start.3 = ((bf16[32,48,128]{2,1,0:T(8,128)(2,1)}), bf16[32,48,128]{2,1,0:T(8,128)(2,1)S(1)}, u32[]{:S(2)}, u32[]{:S(2)}) async-start(bf16[32,48,128]{2,1,0:T(8,128)(2,1)} %mix.1), calls=%async_computation.3 | async-start | bytes 786432 | tf_op jit(solution)/shard_map/all_to_all | solution.py:591
  188.9 10.5 %analyse.3 = bf16[32,48,128]{2,1,0:T(8,128)(2,1)} custom-call(s32[1]{0:T(128)} %bitcast.p_ref, bf16[768,128]{1,0:T(8,128)(2,1)} %get-tuple-element.66.refs_0_, bf16[768,128]{1,0:T(8,128)(2,1)} %copy-done.16, bf16[768,128]{1,0:T(8,128)(2,1)} %copy-done.18, bf16[768,128]{1,0:T(8,128)(2,1)} %copy-done.20, bf16[768,128]{1,0:T(8,128)(2,1)} %copy-done.21, ...), custom_call_target="tpu_custom_call" | custom-call | flops 11000000512 | bytes 10000000 | tf_op jit(solution)/shard_map/analyse/pallas_call | solution.py:25
  202.7 9.4 %synthesise.1 = (bf16[768,128]{1,0:T(8,128)(2,1)}, bf16[768,128]{1,0:T(8,128)(2,1)}, bf16[768,128]{1,0:T(8,128)(2,1)}, bf16[768,128]{1,0:T(8,128)(2,1)}, bf16[76...) custom-call(s32[1]{0:T(128)} %bitcast.p_ref, ...), custom_call_target="tpu_custom_call" | custom-call | flops 11000000512 | bytes 10000000 | tf_op jit(solution)/shard_map/synthesise/pallas_call | solution.py:25
  223.0 5.9 %all-to-all-start.5 = ((bf16[32,48,128]{2,1,0:T(8,128)(2,1)}), bf16[32,48,128]{2,1,0:T(8,128)(2,1)S(1)}, u32[]{:S(2)}, u32[]{:S(2)}) async-start(bf16[32,48,128]{2,1,0:T(8,128)(2,1)} %analyse.3), calls=%async_computation.5 | async-start | bytes 786432 | tf_op jit(solution)/shard_map/all_to_all | solution.py:591
  229.0 6.3 %collective-permute-done.27.refs_3_ = bf16[768,128]{1,0:T(8,128)(2,1)S(1)} collective-permute-done((bf16[768,128]{1,0:T(8,128)(2,1)}, bf16[768,128]{1,0:T(8,128)(2,1)S(1)}, u32[]{:S(2)}, u32[]{:S(2)}) %collective-permute-start.27) | collective-permute-done | bytes 196640 | tf_op jit(solution)/shard_map/ppermute | solution.py:598
  238.4 8.8 %inverse.1 = bf16[32,264,128]{2,1,0:T(8,128)(2,1)} custom-call(s32[1]{0:T(128)} %bitcast.p_ref, bf16[768,128]{1,0:T(8,128)(2,1)} %get-tuple-element.77.refs_0_, bf16[768,128]{1,0:T(8,128)(2,1)} %copy-done.24, bf16[768,128]{1,0:T(8,128)(2,1)} %copy-done.26, bf16[768,128]{1,0:T(8,128)(2,1)} %copy-done.28, bf16[768,128]{1,0:T(8,128)(2,1)} %copy-done.31, ...), custom_call_target="tpu_custom_call" | custom-call | flops 9900000256 | bytes 9000000 | tf_op jit(solution)/shard_map/inverse/pallas_call | solution.py:25
  247.2 5.1 %all-to-all-start.4 = ((bf16[32,264,128]{2,1,0:T(8,128)(2,1)}), bf16[32,264,128]{2,1,0:T(8,128)(2,1)S(1)}, u32[]{:S(2)}, u32[]{:S(2)}) async-start(bf16[32,264,128]{2,1,0:T(8,128)(2,1)} %inverse.1), calls=%async_computation.4 | async-start | bytes 4325376 | tf_op jit(solution)/shard_map/all_to_all | solution.py:591
  252.3 3.4 %grad.1 = (f32[4,3,128,256]{3,2,1,0:T(8,128)}, f32[4,3,128,256]{3,2,1,0:T(8,128)}) custom-call(s32[1]{0:T(128)} %bitcast.p_ref, bf16[32,48,128]{2,1,0:T(8,128)(2,1)} %copy-done.4, bf16[32,48,128]{2,1,0:T(8,128)(2,1)} %copy-done.2), custom_call_target="tpu_custom_call" | custom-call | flops 4400000000 | bytes 4000000 | tf_op jit(solution)/shard_map/grad/pallas_call | solution.py:25
  255.8 3.5 %collective-permute-done.32.b_ref = f32[4,3,128,256]{3,2,1,0:T(8,128)S(1)} collective-permute-done((f32[4,3,128,256]{3,2,1,0:T(8,128)}, f32[4,3,128,256]{3,2,1,0:T(8,128)S(1)}, u32[]{:S(2)}, u32[]{:S(2)}) %collective-permute-start.32) | collective-permute-done | bytes 1572896 | tf_op jit(solution)/shard_map/ppermute | solution.py:609
  267.4 8.2 %collective-permute-done.33.refs_1_ = f32[3,128,256]{2,1,0:T(8,128)S(1)} collective-permute-done((f32[3,128,256]{2,1,0:T(8,128)}, f32[3,128,256]{2,1,0:T(8,128)S(1)}, u32[]{:S(2)}, u32[]{:S(2)}) %collective-permute-start.33) | collective-permute-done | bytes 393248 | tf_op jit(solution)/shard_map/ppermute | solution.py:604
  275.6 9.3 %collective-permute-done.34.refs_2_ = f32[3,128,256]{2,1,0:T(8,128)S(1)} collective-permute-done((f32[3,128,256]{2,1,0:T(8,128)}, f32[3,128,256]{2,1,0:T(8,128)S(1)}, u32[]{:S(2)}, u32[]{:S(2)}) %collective-permute-start.34) | collective-permute-done | bytes 393248 | tf_op jit(solution)/shard_map/ppermute | solution.py:604
  288.0 8.4 %collective-permute-start.36 = (f32[3,32,256]{2,1,0:T(8,128)}, f32[3,32,256]{2,1,0:T(8,128)S(1)}, u32[]{:S(2)}, u32[]{:S(2)}) collective-permute-start(f32[3,32,256]{2,1,0:T(8,128)} %get-tuple-element.93), channel_id=1, source_target_pairs={{0,0},{1,1},{2,2},{3,3},{4,8},{5,9},{6,10},{7,11},{8,4},{9,5},{10,... | collective-permute-start | bytes 294920 | tf_op jit(solution)/shard_map/ppermute | solution.py:621
  297.4 7.8 %collective-permute-start.38 = (f32[3,32,256]{2,1,0:T(8,128)}, f32[3,32,256]{2,1,0:T(8,128)S(1)}, u32[]{:S(2)}, u32[]{:S(2)}) collective-permute-start(f32[3,32,256]{2,1,0:T(8,128)} %get-tuple-element.96), channel_id=1, source_target_pairs={{0,2},{1,3},{2,0},{3,1},{4,10},{5,11},{6,8},{7,9},{8,6},{9,7},{10,... | collective-permute-start | bytes 294920 | tf_op jit(solution)/shard_map/ppermute | solution.py:621
  307.4 4.3 %finish.1 = bf16[22,180,256]{2,1,0:T(8,128)(2,1)} custom-call(s32[1]{0:T(128)} %bitcast.p_ref, bf16[32,264,128]{2,1,0:T(8,128)(2,1)} %copy-done.1, bf16[22,180,256]{2,1,0:T(8,128)(2,1)} %g_ref.1), custom_call_target="tpu_custom_call" | custom-call | flops 4400000000 | bytes 4000000 | tf_op jit(solution)/shard_map/finish/pallas_call | solution.py:25
  (194 shorter events, 78.9 us)
Async XLA Ops:
  5.3 69.4 %all-to-all-start = ((bf16[32,264,128]{2,1,0:T(8,128)(2,1)}), bf16[32,264,128]{2,1,0:T(8,128)(2,1)S(1)}, u32[]{:S(2)}, u32[]{:S(2)}) async-start(bf16[32,264,128]{2,1,0:T(8,128)(2,1)} %pack.2), calls=%async_computation | async-start | bytes 4325376 | tf_op jit(solution)/shard_map/all_to_all | solution.py:591
  17.6 57.1 %collective-permute-start.3 = (bf16[3,32,256]{2,1,0:T(8,128)(2,1)S(1)}, bf16[3,32,256]{2,1,0:T(8,128)(2,1)S(1)}, u32[]{:S(2)}, u32[]{:S(2)}) collective-permute-start(bf16[3,32,256]{2,1,0:T(8,128)(2,1)S(1)} %get-tuple-element.98), channel_id=1, source_target_pairs={{0,3},{1,0},{2,1},{3,2},{4,11},{5,8},{6,9},{7,10},{8,7},{9,4},{10,... | collective-permute-start | bytes 147464 | tf_op jit(solution)/shard_map/ppermute | solution.py:621
  26.0 48.6 %collective-permute-start.2 = (bf16[3,32,256]{2,1,0:T(8,128)(2,1)S(1)}, bf16[3,32,256]{2,1,0:T(8,128)(2,1)S(1)}, u32[]{:S(2)}, u32[]{:S(2)}) collective-permute-start(bf16[3,32,256]{2,1,0:T(8,128)(2,1)S(1)} %get-tuple-element.99), channel_id=1, source_target_pairs={{0,2},{1,3},{2,0},{3,1},{4,10},{5,11},{6,8},{7,9},{8,6},{9,7},{10,... | collective-permute-start | bytes 147464 | tf_op jit(solution)/shard_map/ppermute | solution.py:621
  26.4 48.2 %collective-permute-start.1 = (bf16[3,32,256]{2,1,0:T(8,128)(2,1)S(1)}, bf16[3,32,256]{2,1,0:T(8,128)(2,1)S(1)}, u32[]{:S(2)}, u32[]{:S(2)}) collective-permute-start(bf16[3,32,256]{2,1,0:T(8,128)(2,1)S(1)} %get-tuple-element.100), channel_id=1, source_target_pairs={{0,1},{1,2},{2,3},{3,0},{4,9},{5,10},{6,11},{7,8},{8,5},{9,6},{10,... | collective-permute-start | bytes 147464 | tf_op jit(solution)/shard_map/ppermute | solution.py:621
  32.3 42.3 %collective-permute-start = (bf16[3,32,256]{2,1,0:T(8,128)(2,1)S(1)}, bf16[3,32,256]{2,1,0:T(8,128)(2,1)S(1)}, u32[]{:S(2)}, u32[]{:S(2)}) collective-permute-start(bf16[3,32,256]{2,1,0:T(8,128)(2,1)S(1)} %get-tuple-element.101), channel_id=1, source_target_pairs={{0,0},{1,1},{2,2},{3,3},{4,8},{5,9},{6,10},{7,11},{8,4},{9,5},{10,... | collective-permute-start | bytes 147464 | tf_op jit(solution)/shard_map/ppermute | solution.py:621
  76.2 54.9 %all-to-all-start.1 = ((bf16[32,264,128]{2,1,0:T(8,128)(2,1)}), bf16[32,264,128]{2,1,0:T(8,128)(2,1)}, u32[]{:S(2)}, u32[]{:S(2)}) async-start(bf16[32,264,128]{2,1,0:T(8,128)(2,1)} %pack.3), calls=%async_computation.1 | async-start | bytes 4325376 | tf_op jit(solution)/shard_map/all_to_all | solution.py:591
  98.8 18.0 %collective-permute-start.8 = (bf16[768,128]{1,0:T(8,128)(2,1)}, bf16[768,128]{1,0:T(8,128)(2,1)S(1)}, u32[]{:S(2)}, u32[]{:S(2)}) collective-permute-start(bf16[768,128]{1,0:T(8,128)(2,1)} %get-tuple-element.61), channel_id=1, source_target_pairs={{0,136},{8,128},{64,200},{72,192},{128,8},{136,0},{192,72},{200,64... | collective-permute-start | bytes 589832 | tf_op jit(solution)/shard_map/ppermute | solution.py:598
  100.7 16.1 %collective-permute-start.9 = (bf16[768,128]{1,0:T(8,128)(2,1)}, bf16[768,128]{1,0:T(8,128)(2,1)S(1)}, u32[]{:S(2)}, u32[]{:S(2)}) collective-permute-start(bf16[768,128]{1,0:T(8,128)(2,1)} %get-tuple-element.62), channel_id=1, source_target_pairs={{0,192},{8,200},{64,0},{72,8},{128,64},{136,72},{192,128},{200,136... | collective-permute-start | bytes 589832 | tf_op jit(solution)/shard_map/ppermute | solution.py:598
  134.7 20.7 %collective-permute-start.11 = (bf16[3,128,256]{2,1,0:T(8,128)(2,1)S(1)}, bf16[3,128,256]{2,1,0:T(8,128)(2,1)S(1)}, u32[]{:S(2)}, u32[]{:S(2)}) collective-permute-start(bf16[3,128,256]{2,1,0:T(8,128)(2,1)S(1)} %bitcast.37), channel_id=1, source_target_pairs={{0,8},{8,0},{1,9},{9,1},{2,10},{10,2},{3,11},{11,3},{4,12},{12,4},... | collective-permute-start | bytes 589832 | tf_op jit(solution)/shard_map/ppermute | solution.py:609
  138.0 34.0 %all-to-all-start.2 = ((bf16[32,48,128]{2,1,0:T(8,128)(2,1)}), bf16[32,48,128]{2,1,0:T(8,128)(2,1)S(1)}, u32[]{:S(2)}, u32[]{:S(2)}) async-start(bf16[32,48,128]{2,1,0:T(8,128)(2,1)} %analyse.2), calls=%async_computation.2 | async-start | bytes 786432 | tf_op jit(solution)/shard_map/all_to_all | solution.py:591
  145.0 20.3 %collective-permute-start.17 = (bf16[3,128,256]{2,1,0:T(8,128)(2,1)S(1)}, bf16[3,128,256]{2,1,0:T(8,128)(2,1)S(1)}, u32[]{:S(2)}, u32[]{:S(2)}) collective-permute-start(bf16[3,128,256]{2,1,0:T(8,128)(2,1)S(1)} %collective-permute-done.16.refs_6_), channel_id=1, source_target_pairs={{0,8},{8,0},{1,9},{9,1},{2,10},{10,2},{3,11},{11,3},{4,12},{12,4},... | collective-permute-start | bytes 589832 | tf_op jit(solution)/shard_map/ppermute | solution.py:609
  145.4 20.1 %collective-permute-start.15 = (bf16[3,128,256]{2,1,0:T(8,128)(2,1)S(1)}, bf16[3,128,256]{2,1,0:T(8,128)(2,1)S(1)}, u32[]{:S(2)}, u32[]{:S(2)}) collective-permute-start(bf16[3,128,256]{2,1,0:T(8,128)(2,1)S(1)} %collective-permute-done.14.refs_4_), channel_id=1, source_target_pairs={{0,8},{8,0},{1,9},{9,1},{2,10},{10,2},{3,11},{11,3},{4,12},{12,4},... | collective-permute-start | bytes 589832 | tf_op jit(solution)/shard_map/ppermute | solution.py:609
  145.6 23.0 %collective-permute-start.13 = (bf16[3,128,256]{2,1,0:T(8,128)(2,1)S(1)}, bf16[3,128,256]{2,1,0:T(8,128)(2,1)S(1)}, u32[]{:S(2)}, u32[]{:S(2)}) collective-permute-start(bf16[3,128,256]{2,1,0:T(8,128)(2,1)S(1)} %collective-permute-done.12.refs_2_), channel_id=1, source_target_pairs={{0,8},{8,0},{1,9},{9,1},{2,10},{10,2},{3,11},{11,3},{4,12},{12,4},... | collective-permute-start | bytes 589832 | tf_op jit(solution)/shard_map/ppermute | solution.py:609
  155.3 16.8 %collective-permute-start.18 = (bf16[768,128]{1,0:T(8,128)(2,1)}, bf16[768,128]{1,0:T(8,128)(2,1)S(1)}, u32[]{:S(2)}, u32[]{:S(2)}) collective-permute-start(bf16[768,128]{1,0:T(8,128)(2,1)} %get-tuple-element.69), channel_id=1, source_target_pairs={{0,8},{8,0},{64,72},{72,64},{128,136},{136,128},{192,200},{200,192... | collective-permute-start | bytes 589832 | tf_op jit(solution)/shard_map/ppermute | solution.py:598
  155.4 19.1 %collective-permute-start.19 = (bf16[768,128]{1,0:T(8,128)(2,1)}, bf16[768,128]{1,0:T(8,128)(2,1)S(1)}, u32[]{:S(2)}, u32[]{:S(2)}) collective-permute-start(bf16[768,128]{1,0:T(8,128)(2,1)} %get-tuple-element.70), channel_id=1, source_target_pairs={{0,64},{8,72},{64,128},{72,136},{128,192},{136,200},{192,0},{200,8... | collective-permute-start | bytes 589832 | tf_op jit(solution)/shard_map/ppermute | solution.py:598
  165.4 21.9 %collective-permute-start.20 = (bf16[768,128]{1,0:T(8,128)(2,1)}, bf16[768,128]{1,0:T(8,128)(2,1)S(1)}, u32[]{:S(2)}, u32[]{:S(2)}) collective-permute-start(bf16[768,128]{1,0:T(8,128)(2,1)} %get-tuple-element.71), channel_id=1, source_target_pairs={{0,72},{8,64},{64,136},{72,128},{128,200},{136,192},{192,8},{200,0... | collective-permute-start | bytes 589832 | tf_op jit(solution)/shard_map/ppermute | solution.py:598
  165.6 21.7 %collective-permute-start.21 = (bf16[768,128]{1,0:T(8,128)(2,1)}, bf16[768,128]{1,0:T(8,128)(2,1)S(1)}, u32[]{:S(2)}, u32[]{:S(2)}) collective-permute-start(bf16[768,128]{1,0:T(8,128)(2,1)} %get-tuple-element.72), channel_id=1, source_target_pairs={{0,128},{8,136},{64,192},{72,200},{128,0},{136,8},{192,64},{200,72... | collective-permute-start | bytes 589832 | tf_op jit(solution)/shard_map/ppermute | solution.py:598
  168.7 18.7 %collective-permute-start.22 = (bf16[768,128]{1,0:T(8,128)(2,1)}, bf16[768,128]{1,0:T(8,128)(2,1)S(1)}, u32[]{:S(2)}, u32[]{:S(2)}) collective-permute-start(bf16[768,128]{1,0:T(8,128)(2,1)} %get-tuple-element.73), channel_id=1, source_target_pairs={{0,136},{8,128},{64,200},{72,192},{128,8},{136,0},{192,72},{200,64... | collective-permute-start | bytes 589832 | tf_op jit(solution)/shard_map/ppermute | solution.py:598
  172.1 15.3 %collective-permute-start.23 = (bf16[768,128]{1,0:T(8,128)(2,1)S(1)}, bf16[768,128]{1,0:T(8,128)(2,1)S(1)}, u32[]{:S(2)}, u32[]{:S(2)}) collective-permute-start(bf16[768,128]{1,0:T(8,128)(2,1)S(1)} %copy-done.17), channel_id=1, source_target_pairs={{0,192},{8,200},{64,0},{72,8},{128,64},{136,72},{192,128},{200,136... | collective-permute-start | bytes 589832 | tf_op jit(solution)/shard_map/ppermute | solution.py:598
  178.3 23.6 %all-to-all-start.3 = ((bf16[32,48,128]{2,1,0:T(8,128)(2,1)}), bf16[32,48,128]{2,1,0:T(8,128)(2,1)S(1)}, u32[]{:S(2)}, u32[]{:S(2)}) async-start(bf16[32,48,128]{2,1,0:T(8,128)(2,1)} %mix.1), calls=%async_computation.3 | async-start | bytes 786432 | tf_op jit(solution)/shard_map/all_to_all | solution.py:591
  215.8 19.5 %collective-permute-start.27 = (bf16[768,128]{1,0:T(8,128)(2,1)}, bf16[768,128]{1,0:T(8,128)(2,1)S(1)}, u32[]{:S(2)}, u32[]{:S(2)}) collective-permute-start(bf16[768,128]{1,0:T(8,128)(2,1)} %get-tuple-element.80), channel_id=1, source_target_pairs={{0,72},{8,64},{64,136},{72,128},{128,200},{136,192},{192,8},{200,0... | collective-permute-start | bytes 589832 | tf_op jit(solution)/shard_map/ppermute | solution.py:598
  215.9 19.4 %collective-permute-start.28 = (bf16[768,128]{1,0:T(8,128)(2,1)}, bf16[768,128]{1,0:T(8,128)(2,1)S(1)}, u32[]{:S(2)}, u32[]{:S(2)}) collective-permute-start(bf16[768,128]{1,0:T(8,128)(2,1)} %get-tuple-element.81), channel_id=1, source_target_pairs={{0,128},{8,136},{64,192},{72,200},{128,0},{136,8},{192,64},{200,72... | collective-permute-start | bytes 589832 | tf_op jit(solution)/shard_map/ppermute | solution.py:598
  218.4 16.9 %collective-permute-start.29 = (bf16[768,128]{1,0:T(8,128)(2,1)}, bf16[768,128]{1,0:T(8,128)(2,1)S(1)}, u32[]{:S(2)}, u32[]{:S(2)}) collective-permute-start(bf16[768,128]{1,0:T(8,128)(2,1)} %get-tuple-element.82), channel_id=1, source_target_pairs={{0,136},{8,128},{64,200},{72,192},{128,8},{136,0},{192,72},{200,64... | collective-permute-start | bytes 589832 | tf_op jit(solution)/shard_map/ppermute | solution.py:598
  219.4 15.9 %collective-permute-start.30 = (bf16[768,128]{1,0:T(8,128)(2,1)}, bf16[768,128]{1,0:T(8,128)(2,1)S(1)}, u32[]{:S(2)}, u32[]{:S(2)}) collective-permute-start(bf16[768,128]{1,0:T(8,128)(2,1)} %get-tuple-element.83), channel_id=1, source_target_pairs={{0,192},{8,200},{64,0},{72,8},{128,64},{136,72},{192,128},{200,136... | collective-permute-start | bytes 589832 | tf_op jit(solution)/shard_map/ppermute | solution.py:598
  222.2 15.4 %collective-permute-start.31 = (bf16[768,128]{1,0:T(8,128)(2,1)}, bf16[768,128]{1,0:T(8,128)(2,1)S(1)}, u32[]{:S(2)}, u32[]{:S(2)}) collective-permute-start(bf16[768,128]{1,0:T(8,128)(2,1)} %get-tuple-element.84), channel_id=1, source_target_pairs={{0,200},{8,192},{64,8},{72,0},{128,72},{136,64},{192,136},{200,128... | collective-permute-start | bytes 589832 | tf_op jit(solution)/shard_map/ppermute | solution.py:598
  223.0 24.1 %all-to-all-start.5 = ((bf16[32,48,128]{2,1,0:T(8,128)(2,1)}), bf16[32,48,128]{2,1,0:T(8,128)(2,1)S(1)}, u32[]{:S(2)}, u32[]{:S(2)}) async-start(bf16[32,48,128]{2,1,0:T(8,128)(2,1)} %analyse.3), calls=%async_computation.5 | async-start | bytes 786432 | tf_op jit(solution)/shard_map/all_to_all | solution.py:591
  247.2 58.9 %all-to-all-start.4 = ((bf16[32,264,128]{2,1,0:T(8,128)(2,1)}), bf16[32,264,128]{2,1,0:T(8,128)(2,1)S(1)}, u32[]{:S(2)}, u32[]{:S(2)}) async-start(bf16[32,264,128]{2,1,0:T(8,128)(2,1)} %inverse.1), calls=%async_computation.4 | async-start | bytes 4325376 | tf_op jit(solution)/shard_map/all_to_all | solution.py:591
  264.5 20.3 %collective-permute-start.34 = (f32[3,128,256]{2,1,0:T(8,128)}, f32[3,128,256]{2,1,0:T(8,128)S(1)}, u32[]{:S(2)}, u32[]{:S(2)}) collective-permute-start(f32[3,128,256]{2,1,0:T(8,128)} %get-tuple-element.91), channel_id=1, source_target_pairs={{0,128},{64,192},{128,0},{192,64},{1,129},{65,193},{129,1},{193,65... | collective-permute-start | bytes 1179656 | tf_op jit(solution)/shard_map/ppermute | solution.py:604
  267.4 17.5 %collective-permute-start.35 = (f32[3,128,256]{2,1,0:T(8,128)}, f32[3,128,256]{2,1,0:T(8,128)S(1)}, u32[]{:S(2)}, u32[]{:S(2)}) collective-permute-start(f32[3,128,256]{2,1,0:T(8,128)} %get-tuple-element.92), channel_id=1, source_target_pairs={{0,192},{64,0},{128,64},{192,128},{1,193},{65,1},{129,65},{193,129... | collective-permute-start | bytes 1179656 | tf_op jit(solution)/shard_map/ppermute | solution.py:604
  288.0 23.7 %collective-permute-start.36 = (f32[3,32,256]{2,1,0:T(8,128)}, f32[3,32,256]{2,1,0:T(8,128)S(1)}, u32[]{:S(2)}, u32[]{:S(2)}) collective-permute-start(f32[3,32,256]{2,1,0:T(8,128)} %get-tuple-element.93), channel_id=1, source_target_pairs={{0,0},{1,1},{2,2},{3,3},{4,8},{5,9},{6,10},{7,11},{8,4},{9,5},{10,... | collective-permute-start | bytes 294920 | tf_op jit(solution)/shard_map/ppermute | solution.py:621
  296.4 15.3 %collective-permute-start.37 = (f32[3,32,256]{2,1,0:T(8,128)}, f32[3,32,256]{2,1,0:T(8,128)S(1)}, u32[]{:S(2)}, u32[]{:S(2)}) collective-permute-start(f32[3,32,256]{2,1,0:T(8,128)} %get-tuple-element.95), channel_id=1, source_target_pairs={{0,1},{1,2},{2,3},{3,0},{4,9},{5,10},{6,11},{7,8},{8,5},{9,6},{10,... | collective-permute-start | bytes 294920 | tf_op jit(solution)/shard_map/ppermute | solution.py:621
  297.4 15.2 %collective-permute-start.38 = (f32[3,32,256]{2,1,0:T(8,128)}, f32[3,32,256]{2,1,0:T(8,128)S(1)}, u32[]{:S(2)}, u32[]{:S(2)}) collective-permute-start(f32[3,32,256]{2,1,0:T(8,128)} %get-tuple-element.96), channel_id=1, source_target_pairs={{0,2},{1,3},{2,0},{3,1},{4,10},{5,11},{6,8},{7,9},{8,6},{9,7},{10,... | collective-permute-start | bytes 294920 | tf_op jit(solution)/shard_map/ppermute | solution.py:621
  (56 other events, 416.8 us)
where the time goes:
time: 321 us; the launch traced here: 315 us
  starting transfers between devices  134 us (42%)
  Pallas kernels  112 us (35%)
  waiting for transfers between devices  50.3 us (16%)
  local copies, waits for them, and re-layouts  12 us (4%)
  other arithmetic  6.02 us (2%)
    pallas_call x16, Pallas kernels, call(): pl.pallas_call(body, out_shape=outs, grid=grid, in_specs=[whole(a) if s i...  112 us
    all_to_all x6, starting transfers between devices, swap(): return lax.all_to_all(value, RING, split_axis=0, concat_axis=0, tiled=True)  45.2 us
    ppermute x21, starting transfers between devices, cross(): moved.append(lax.ppermute(pieces[k], CROSS, pairs))  41.7 us
    ppermute x8, starting transfers between devices, turned(): moved.append(lax.ppermute(piece, ('core', 'zhi', 'y'), pairs))  34.6 us
    ppermute x21, waiting for transfers between devices, cross(): moved.append(lax.ppermute(pieces[k], CROSS, pairs))  22.1 us
    ppermute x6, waiting for transfers between devices, along_x(): lax.ppermute(pieces[dx], 'x', [(i, (i + dx) % 4) for i in range(4)])  17.5 us
    unnamed x84, local copies, waits for them, and re-layouts  8.6 us
    ppermute x6, starting transfers between devices, along_x(): lax.ppermute(pieces[dx], 'x', [(i, (i + dx) % 4) for i in range(4)])  7.39 us
  transfers between devices with their start and end apart: 46, of which 14 were waited for; matrix products, arithmetic and copies ran while one was open for 3% of the time, Pallas kernels for 31%

commit v1 on v0

--- a/solution.py
+++ b/solution.py
@@ -159,7 +159,7 @@
         o_refs[k][...] = t_ref[pl.ds(start, 768), :].astype(BF16)
 
 
-def fourier(position, received, table, weights):
+def fourier(position, received, table, weights, us):
     return call(
         fourier_kernel,
         (PIECE,) * 8,
@@ -170,7 +170,7 @@
             pltpu.VMEM((6144, 128), F32),
         ],
         specs=[SMEM, None, None, None],
-        us=9,
+        us=us,
         name="fourier",
     )
 
@@ -201,18 +201,21 @@
     def steps(n, carried):
         previous, earlier, scale = carried
         size = jnp.exp(scale)
+        first = jnp.full((8, 128), part * 128 + n * 8, jnp.int32).astype(F32)
+
+        def ratios(degree):
+            above = jnp.maximum(4.0 * degree * degree - 1.0, 0.0)
+            below = jnp.maximum(degree * degree - square, 0.0)
+            root = lax.rsqrt(jnp.maximum(above * below, 1e-6))
+            return above * root, below * root
+
+        _, shrink = ratios(jnp.maximum(first - 1.0, 0.0))
         for u in range(8):
             l = n * 8 + u
-            degree = jnp.full((8, 128), part * 128 + l, jnp.int32).astype(F32)
-            below = (degree - 1.0) * (degree - 1.0)
-            growth = jnp.sqrt(
-                jnp.maximum(4.0 * degree * degree - 1.0, 0.0)
-                / jnp.maximum(degree * degree - square, 1.0)
-            )
-            shrink = jnp.sqrt(
-                jnp.maximum(below - square, 0.0) / jnp.maximum(4.0 * below - 1.0, 1.0)
-            )
+            degree = first + float(u)
+            growth, inverse_growth = ratios(degree)
             current = wide(growth) * (cosine * previous) - wide(growth * shrink) * earlier
+            shrink = inverse_growth
             current = jnp.where(wide(degree == order), 1.0, current)
             value = current * size
             for d in range(4):
@@ -440,7 +443,7 @@
         jax.ShapeDtypeStruct((8, 3, 128, CH), BF16),
         [position, *pieces],
         specs=[SMEM] + [None] * 8,
-        us=2,
+        us=1,
         name="gather",
     )
 
@@ -680,13 +683,13 @@
     own = lax.dynamic_slice_in_dim(quadrature, position * 128, 128)
     sent_g = after(sent_g, packed_x, forward, backward, table, weights)
     sent_x = swap(after(packed_x, sent_g))
-    pieces_g = fourier(where, sent_g, backward, jnp.ones((8, 128), F32))
+    pieces_g = fourier(where, sent_g, backward, jnp.ones((8, 128), F32), 9)
     packed_adjoint = analyse(where, cross(pieces_g), table)
     adjoint = swap(after(packed_adjoint, sent_x))
     weights = along_x([after(weights, packed_adjoint, sent_x)] * 4)
     weights = [w for near in weights for w in (near, other_core(near))]
     weights = gather(where, weights).reshape(4, 2, 3, 128, CH)
-    pieces_x = fourier(where, sent_x, forward, jnp.broadcast_to(own[None, :], (8, 128)))
+    pieces_x = fourier(where, sent_x, forward, jnp.broadcast_to(own[None, :], (8, 128)), 1)
     mixed = swap(mix(after(adjoint, pieces_x[0]), weights))
     coefficients = analyse(where, cross(pieces_x), table)
     mixed = after(mixed, coefficients)

time: 321 us -> 326 us (1.016)
  waiting for transfers between devices: 50.3 us -> 57 us
  Pallas kernels: 112 us -> 108 us
    ppermute x5, starting transfers between devices: 4.93 us -> 10.4 us  [other_core(): return lax.ppermute(value, 'core', [(0, 1), (1, 0)])]
    ppermute x21, starting transfers between devices: 41.7 us -> 37.3 us  [cross(): moved.append(lax.ppermute(pieces[k], CROSS, pairs))]
    pallas_call x16, Pallas kernels: 112 us -> 108 us  [call(): pl.pallas_call(body, out_shape=outs, grid=grid, in_specs=[whole(a) if s i...]
    unnamed x84 -> x80, local copies, waits for them, and re-layouts: 8.6 us -> 8.66 us
  transfers between devices with their start and end apart: 46 -> 46, of which waited for: 14 -> 19; matrix products, arithmetic and copies ran while one was open for 3% -> 3% of each run, Pallas kernels for 31% -> 29%
where the time goes in v1:
time: 326 us; the launch traced here: 320 us
  starting transfers between devices  136 us (42%)
  Pallas kernels  108 us (33%)
  waiting for transfers between devices  57 us (17%)
  local copies, waits for them, and re-layouts  12 us (4%)
  other arithmetic  6.02 us (2%)
    pallas_call x16, Pallas kernels, call(): pl.pallas_call(body, out_shape=outs, grid=grid, in_specs=[whole(a) if s i...  108 us
    all_to_all x6, starting transfers between devices, swap(): return lax.all_to_all(value, RING, split_axis=0, concat_axis=0, tiled=True)  46 us
    ppermute x21, starting transfers between devices, cross(): moved.append(lax.ppermute(pieces[k], CROSS, pairs))  37.3 us
    ppermute x8, starting transfers between devices, turned(): moved.append(lax.ppermute(piece, ('core', 'zhi', 'y'), pairs))  34.6 us
    ppermute x21, waiting for transfers between devices, cross(): moved.append(lax.ppermute(pieces[k], CROSS, pairs))  22.7 us
    ppermute x6, waiting for transfers between devices, along_x(): lax.ppermute(pieces[dx], 'x', [(i, (i + dx) % 4) for i in range(4)])  19.1 us
    ppermute x5, starting transfers between devices, other_core(): return lax.ppermute(value, 'core', [(0, 1), (1, 0)])  10.4 us
    unnamed x80, local copies, waits for them, and re-layouts  8.66 us
  transfers between devices with their start and end apart: 46, of which 19 were waited for; matrix products, arithmetic and copies ran while one was open for 3% of the time, Pallas kernels for 29%

profile of v1, /device:TPU:1, one launch (start us, length us, event | category | flops | bytes accessed | tf_op | source)
XLA Modules:
  0.0 320.1 jit_solution(11697457664867286616)
XLA Ops:
  0.6 4.7 %pack.2 = bf16[32,264,128]{2,1,0:T(8,128)(2,1)} custom-call(s32[1]{0:T(128)} %bitcast.p_ref, bf16[22,180,256]{2,1,0:T(8,128)(2,1)} %g_ref.1), custom_call_target="tpu_custom_call" | custom-call | flops 5500000256 | bytes 5000000 | tf_op jit(solution)/shard_map/pack/pallas_call | solution.py:25
  5.3 12.2 %all-to-all-start = ((bf16[32,264,128]{2,1,0:T(8,128)(2,1)}), bf16[32,264,128]{2,1,0:T(8,128)(2,1)S(1)}, u32[]{:S(2)}, u32[]{:S(2)}) async-start(bf16[32,264,128]{2,1,0:T(8,128)(2,1)} %pack.2), calls=%async_computation | async-start | bytes 4325376 | tf_op jit(solution)/shard_map/all_to_all | solution.py:594
  17.6 8.4 %collective-permute-start.3 = (bf16[3,32,256]{2,1,0:T(8,128)(2,1)S(1)}, bf16[3,32,256]{2,1,0:T(8,128)(2,1)S(1)}, u32[]{:S(2)}, u32[]{:S(2)}) collective-permute-start(bf16[3,32,256]{2,1,0:T(8,128)(2,1)S(1)} %get-tuple-element.98), channel_id=1, source_target_pairs={{0,3},{1,0},{2,1},{3,2},{4,11},{5,8},{6,9},{7,10},{8,7},{9,4},{10,... | collective-permute-start | bytes 147464 | tf_op jit(solution)/shard_map/ppermute | solution.py:624
  26.4 5.8 %collective-permute-start.1 = (bf16[3,32,256]{2,1,0:T(8,128)(2,1)S(1)}, bf16[3,32,256]{2,1,0:T(8,128)(2,1)S(1)}, u32[]{:S(2)}, u32[]{:S(2)}) collective-permute-start(bf16[3,32,256]{2,1,0:T(8,128)(2,1)S(1)} %get-tuple-element.100), channel_id=1, source_target_pairs={{0,1},{1,2},{2,3},{3,0},{4,9},{5,10},{6,11},{7,8},{8,5},{9,6},{10,... | collective-permute-start | bytes 147464 | tf_op jit(solution)/shard_map/ppermute | solution.py:624
  34.6 4.6 %pack.3 = bf16[32,264,128]{2,1,0:T(8,128)(2,1)} custom-call(s32[1]{0:T(128)} %bitcast.p_ref, bf16[22,180,256]{2,1,0:T(8,128)(2,1)} %x_ref.2), custom_call_target="tpu_custom_call" | custom-call | flops 5500000256 | bytes 5000000 | tf_op jit(solution)/shard_map/pack/pallas_call | solution.py:25
  40.7 5.0 %sine_select_fusion = (f32[768,256]{1,0:T(8,128)}, f32[768,256]{1,0:T(8,128)}) fusion(s32[768]{0:T(1024)S(1)} %get-tuple-element.108, s32[768]{0:T(1024)S(1)} %get-tuple-element.107, s32[256]{0:T(256)S(1)} %compare_select_fusion, pred[256]{0:T(512)(128)(4,1)S(1)} %broadcast_compare_fusion.1), kind=kLoop, calls=%fused_computation.3 | loop fusion | flops 2359296 | bytes 1580288 | tf_op jit(solution)/shard_map/jit(_where)/select_n | solution.py:115
  46.2 19.9 %legendre.1.refs_8_.refs_9_.refs_10_.refs_0_.refs_1_.refs_2_ = bf16[12,8,128,512]{3,2,1,0:T(8,128)(2,1)} custom-call(f32[48,128]{1,0:T(8,128)} %broadcast_in_dim.123.m_ref, f32[8,512]{1,0:T(8,128)} %broadcast_in_dim.125.cos_ref, f32[48,512]{1,0:T(8,128)} %add_select_fusion.1.log_ref), custom_call_target="tpu_custom_call" | custom-call | flops 27499999232 | bytes 25000000 | tf_op jit(solution)/shard_map/legendre/pallas_call | solution.py:25
  66.1 4.5 %waves.1 = (bf16[768,1536]{1,0:T(8,128)(2,1)}, bf16[768,1536]{1,0:T(8,128)(2,1)}) custom-call(f32[768,256]{1,0:T(8,128)} %get-tuple-element.103.c_ref, f32[768,256]{1,0:T(8,128)} %get-tuple-element.102.s_ref), custom_call_target="tpu_custom_call" | custom-call | flops 4400000000 | bytes 4000000 | tf_op jit(solution)/shard_map/waves/pallas_call | solution.py:25
  74.1 6.1 %all-to-all-start.1 = ((bf16[32,264,128]{2,1,0:T(8,128)(2,1)}), bf16[32,264,128]{2,1,0:T(8,128)(2,1)S(1)}, u32[]{:S(2)}, u32[]{:S(2)}) async-start(bf16[32,264,128]{2,1,0:T(8,128)(2,1)} %pack.3), calls=%async_computation.1 | async-start | bytes 4325376 | tf_op jit(solution)/shard_map/all_to_all | solution.py:594
  80.8 8.1 %fourier.2 = (bf16[768,128]{1,0:T(8,128)(2,1)}, bf16[768,128]{1,0:T(8,128)(2,1)}, bf16[768,128]{1,0:T(8,128)(2,1)}, bf16[768,128]{1,0:T(8,128)(2,1)}, bf16[768,1...) custom-call(s32[1]{0:T(128)} %bitcast.p_ref, ...), custom_call_target="tpu_custom_call" | custom-call | flops 9900000256 | bytes 9000000 | tf_op jit(solution)/shard_map/fourier/pallas_call | solution.py:25
  103.1 4.7 %collective-permute-done.7.refs_4_ = bf16[768,128]{1,0:T(8,128)(2,1)S(1)} collective-permute-done((bf16[768,128]{1,0:T(8,128)(2,1)}, bf16[768,128]{1,0:T(8,128)(2,1)S(1)}, u32[]{:S(2)}, u32[]{:S(2)}) %collective-permute-start.7) | collective-permute-done | bytes 196640 | tf_op jit(solution)/shard_map/ppermute | solution.py:601
  107.8 4.7 %collective-permute-done.8.refs_5_ = bf16[768,128]{1,0:T(8,128)(2,1)S(1)} collective-permute-done((bf16[768,128]{1,0:T(8,128)(2,1)}, bf16[768,128]{1,0:T(8,128)(2,1)S(1)}, u32[]{:S(2)}, u32[]{:S(2)}) %collective-permute-start.8) | collective-permute-done | bytes 196640 | tf_op jit(solution)/shard_map/ppermute | solution.py:601
  114.2 10.5 %analyse.2 = bf16[32,48,128]{2,1,0:T(8,128)(2,1)} custom-call(s32[1]{0:T(128)} %bitcast.p_ref, bf16[768,128]{1,0:T(8,128)(2,1)} %get-tuple-element.56.refs_0_, bf16[768,128]{1,0:T(8,128)(2,1)} %copy-done.26, bf16[768,128]{1,0:T(8,128)(2,1)} %copy-done.28, bf16[768,128]{1,0:T(8,128)(2,1)} %copy-done.30, bf16[768,128]{1,0:T(8,128)(2,1)} %copy-done.32, ...), custom_call_target="tpu_custom_call" | custom-call | flops 11000000512 | bytes 10000000 | tf_op jit(solution)/shard_map/analyse/pallas_call | solution.py:25
  124.8 3.9 %all-to-all-done.1.r_ref = bf16[32,264,128]{2,1,0:T(8,128)(2,1)S(1)} async-done(((bf16[32,264,128]{2,1,0:T(8,128)(2,1)}), bf16[32,264,128]{2,1,0:T(8,128)(2,1)S(1)}, u32[]{:S(2)}, u32[]{:S(2)}) %all-to-all-start.1) | async-done | bytes 2162720 | tf_op jit(solution)/shard_map/all_to_all | solution.py:594
  128.7 8.1 %all-to-all-start.2 = ((bf16[32,48,128]{2,1,0:T(8,128)(2,1)}), bf16[32,48,128]{2,1,0:T(8,128)(2,1)S(1)}, u32[]{:S(2)}, u32[]{:S(2)}) async-start(bf16[32,48,128]{2,1,0:T(8,128)(2,1)} %analyse.2), calls=%async_computation.2 | async-start | bytes 786432 | tf_op jit(solution)/shard_map/all_to_all | solution.py:594
  144.0 4.7 %collective-permute-start.17 = (bf16[3,128,256]{2,1,0:T(8,128)(2,1)S(1)}, bf16[3,128,256]{2,1,0:T(8,128)(2,1)}, u32[]{:S(2)}, u32[]{:S(2)}) collective-permute-start(bf16[3,128,256]{2,1,0:T(8,128)(2,1)S(1)} %collective-permute-done.16.refs_6_), channel_id=1, source_target_pairs={{0,8},{8,0},{1,9},{9,1},{2,10},{10,2},{3,11},{11,3},{4,12},{12,4},... | collective-permute-start | bytes 589832 | tf_op jit(solution)/shard_map/ppermute | solution.py:612
  153.1 8.1 %fourier.3 = (bf16[768,128]{1,0:T(8,128)(2,1)}, bf16[768,128]{1,0:T(8,128)(2,1)}, bf16[768,128]{1,0:T(8,128)(2,1)}, bf16[768,128]{1,0:T(8,128)(2,1)}, bf16[768,1...) custom-call(s32[1]{0:T(128)} %bitcast.p_ref, ...), custom_call_target="tpu_custom_call" | custom-call | flops 1100000000 | bytes 1000000 | tf_op jit(solution)/shard_map/fourier/pallas_call | solution.py:25
  161.3 9.0 %collective-permute-start.19 = (bf16[768,128]{1,0:T(8,128)(2,1)}, bf16[768,128]{1,0:T(8,128)(2,1)S(1)}, u32[]{:S(2)}, u32[]{:S(2)}) collective-permute-start(bf16[768,128]{1,0:T(8,128)(2,1)} %get-tuple-element.70), channel_id=1, source_target_pairs={{0,64},{8,72},{64,128},{72,136},{128,192},{136,200},{192,0},{200,8... | collective-permute-start | bytes 589832 | tf_op jit(solution)/shard_map/ppermute | solution.py:601
  170.8 3.7 %collective-permute-start.21 = (bf16[768,128]{1,0:T(8,128)(2,1)}, bf16[768,128]{1,0:T(8,128)(2,1)S(1)}, u32[]{:S(2)}, u32[]{:S(2)}) collective-permute-start(bf16[768,128]{1,0:T(8,128)(2,1)} %get-tuple-element.72), channel_id=1, source_target_pairs={{0,128},{8,136},{64,192},{72,200},{128,0},{136,8},{192,64},{200,72... | collective-permute-start | bytes 589832 | tf_op jit(solution)/shard_map/ppermute | solution.py:601
  184.1 9.3 %all-to-all-start.3 = ((bf16[32,48,128]{2,1,0:T(8,128)(2,1)}), bf16[32,48,128]{2,1,0:T(8,128)(2,1)S(1)}, u32[]{:S(2)}, u32[]{:S(2)}) async-start(bf16[32,48,128]{2,1,0:T(8,128)(2,1)} %mix.1), calls=%async_computation.3 | async-start | bytes 786432 | tf_op jit(solution)/shard_map/all_to_all | solution.py:594
  195.0 10.5 %analyse.3 = bf16[32,48,128]{2,1,0:T(8,128)(2,1)} custom-call(s32[1]{0:T(128)} %bitcast.p_ref, bf16[768,128]{1,0:T(8,128)(2,1)} %get-tuple-element.66.refs_0_, bf16[768,128]{1,0:T(8,128)(2,1)} %copy-done.16, bf16[768,128]{1,0:T(8,128)(2,1)} %copy-done.20, bf16[768,128]{1,0:T(8,128)(2,1)} %copy-done.21, bf16[768,128]{1,0:T(8,128)(2,1)} %copy-done.22, ...), custom_call_target="tpu_custom_call" | custom-call | flops 11000000512 | bytes 10000000 | tf_op jit(solution)/shard_map/analyse/pallas_call | solution.py:25
  209.4 9.4 %synthesise.1 = (bf16[768,128]{1,0:T(8,128)(2,1)}, bf16[768,128]{1,0:T(8,128)(2,1)}, bf16[768,128]{1,0:T(8,128)(2,1)}, bf16[768,128]{1,0:T(8,128)(2,1)}, bf16[76...) custom-call(s32[1]{0:T(128)} %bitcast.p_ref, ...), custom_call_target="tpu_custom_call" | custom-call | flops 11000000512 | bytes 10000000 | tf_op jit(solution)/shard_map/synthesise/pallas_call | solution.py:25
  220.4 4.1 %collective-permute-start.28 = (bf16[768,128]{1,0:T(8,128)(2,1)}, bf16[768,128]{1,0:T(8,128)(2,1)S(1)}, u32[]{:S(2)}, u32[]{:S(2)}) collective-permute-start(bf16[768,128]{1,0:T(8,128)(2,1)} %get-tuple-element.81), channel_id=1, source_target_pairs={{0,128},{8,136},{64,192},{72,200},{128,0},{136,8},{192,64},{200,72... | collective-permute-start | bytes 589832 | tf_op jit(solution)/shard_map/ppermute | solution.py:601
  228.9 5.1 %all-to-all-start.5 = ((bf16[32,48,128]{2,1,0:T(8,128)(2,1)}), bf16[32,48,128]{2,1,0:T(8,128)(2,1)S(1)}, u32[]{:S(2)}, u32[]{:S(2)}) async-start(bf16[32,48,128]{2,1,0:T(8,128)(2,1)} %analyse.3), calls=%async_computation.5 | async-start | bytes 786432 | tf_op jit(solution)/shard_map/all_to_all | solution.py:594
  233.9 7.4 %collective-permute-done.27.refs_3_ = bf16[768,128]{1,0:T(8,128)(2,1)S(1)} collective-permute-done((bf16[768,128]{1,0:T(8,128)(2,1)}, bf16[768,128]{1,0:T(8,128)(2,1)S(1)}, u32[]{:S(2)}, u32[]{:S(2)}) %collective-permute-start.27) | collective-permute-done | bytes 196640 | tf_op jit(solution)/shard_map/ppermute | solution.py:601
  243.0 8.8 %inverse.1 = bf16[32,264,128]{2,1,0:T(8,128)(2,1)} custom-call(s32[1]{0:T(128)} %bitcast.p_ref, bf16[768,128]{1,0:T(8,128)(2,1)} %get-tuple-element.77.refs_0_, bf16[768,128]{1,0:T(8,128)(2,1)} %copy-done.24, bf16[768,128]{1,0:T(8,128)(2,1)} %copy-done.25, bf16[768,128]{1,0:T(8,128)(2,1)} %copy-done.27, bf16[768,128]{1,0:T(8,128)(2,1)} %copy-done.29, ...), custom_call_target="tpu_custom_call" | custom-call | flops 9900000256 | bytes 9000000 | tf_op jit(solution)/shard_map/inverse/pallas_call | solution.py:25
  251.7 5.3 %all-to-all-start.4 = ((bf16[32,264,128]{2,1,0:T(8,128)(2,1)}), bf16[32,264,128]{2,1,0:T(8,128)(2,1)S(1)}, u32[]{:S(2)}, u32[]{:S(2)}) async-start(bf16[32,264,128]{2,1,0:T(8,128)(2,1)} %inverse.1), calls=%async_computation.4 | async-start | bytes 4325376 | tf_op jit(solution)/shard_map/all_to_all | solution.py:594
  272.1 8.2 %collective-permute-done.33.refs_1_ = f32[3,128,256]{2,1,0:T(8,128)S(1)} collective-permute-done((f32[3,128,256]{2,1,0:T(8,128)}, f32[3,128,256]{2,1,0:T(8,128)S(1)}, u32[]{:S(2)}, u32[]{:S(2)}) %collective-permute-start.33) | collective-permute-done | bytes 393248 | tf_op jit(solution)/shard_map/ppermute | solution.py:607
  280.3 9.3 %collective-permute-done.34.refs_2_ = f32[3,128,256]{2,1,0:T(8,128)S(1)} collective-permute-done((f32[3,128,256]{2,1,0:T(8,128)}, f32[3,128,256]{2,1,0:T(8,128)S(1)}, u32[]{:S(2)}, u32[]{:S(2)}) %collective-permute-start.34) | collective-permute-done | bytes 393248 | tf_op jit(solution)/shard_map/ppermute | solution.py:607
  292.7 8.4 %collective-permute-start.36 = (f32[3,32,256]{2,1,0:T(8,128)}, f32[3,32,256]{2,1,0:T(8,128)S(1)}, u32[]{:S(2)}, u32[]{:S(2)}) collective-permute-start(f32[3,32,256]{2,1,0:T(8,128)} %get-tuple-element.93), channel_id=1, source_target_pairs={{0,0},{1,1},{2,2},{3,3},{4,8},{5,9},{6,10},{7,11},{8,4},{9,5},{10,... | collective-permute-start | bytes 294920 | tf_op jit(solution)/shard_map/ppermute | solution.py:624
  302.1 7.8 %collective-permute-start.38 = (f32[3,32,256]{2,1,0:T(8,128)}, f32[3,32,256]{2,1,0:T(8,128)S(1)}, u32[]{:S(2)}, u32[]{:S(2)}) collective-permute-start(f32[3,32,256]{2,1,0:T(8,128)} %get-tuple-element.96), channel_id=1, source_target_pairs={{0,2},{1,3},{2,0},{3,1},{4,10},{5,11},{6,8},{7,9},{8,6},{9,7},{10,... | collective-permute-start | bytes 294920 | tf_op jit(solution)/shard_map/ppermute | solution.py:624
  312.1 4.3 %finish.1 = bf16[22,180,256]{2,1,0:T(8,128)(2,1)} custom-call(s32[1]{0:T(128)} %bitcast.p_ref, bf16[32,264,128]{2,1,0:T(8,128)(2,1)} %copy-done.2, bf16[22,180,256]{2,1,0:T(8,128)(2,1)} %g_ref.1), custom_call_target="tpu_custom_call" | custom-call | flops 4400000000 | bytes 4000000 | tf_op jit(solution)/shard_map/finish/pallas_call | solution.py:25
  (190 shorter events, 84.2 us)
Async XLA Ops:
  5.3 67.4 %all-to-all-start = ((bf16[32,264,128]{2,1,0:T(8,128)(2,1)}), bf16[32,264,128]{2,1,0:T(8,128)(2,1)S(1)}, u32[]{:S(2)}, u32[]{:S(2)}) async-start(bf16[32,264,128]{2,1,0:T(8,128)(2,1)} %pack.2), calls=%async_computation | async-start | bytes 4325376 | tf_op jit(solution)/shard_map/all_to_all | solution.py:594
  17.6 55.1 %collective-permute-start.3 = (bf16[3,32,256]{2,1,0:T(8,128)(2,1)S(1)}, bf16[3,32,256]{2,1,0:T(8,128)(2,1)S(1)}, u32[]{:S(2)}, u32[]{:S(2)}) collective-permute-start(bf16[3,32,256]{2,1,0:T(8,128)(2,1)S(1)} %get-tuple-element.98), channel_id=1, source_target_pairs={{0,3},{1,0},{2,1},{3,2},{4,11},{5,8},{6,9},{7,10},{8,7},{9,4},{10,... | collective-permute-start | bytes 147464 | tf_op jit(solution)/shard_map/ppermute | solution.py:624
  26.0 46.6 %collective-permute-start.2 = (bf16[3,32,256]{2,1,0:T(8,128)(2,1)S(1)}, bf16[3,32,256]{2,1,0:T(8,128)(2,1)S(1)}, u32[]{:S(2)}, u32[]{:S(2)}) collective-permute-start(bf16[3,32,256]{2,1,0:T(8,128)(2,1)S(1)} %get-tuple-element.99), channel_id=1, source_target_pairs={{0,2},{1,3},{2,0},{3,1},{4,10},{5,11},{6,8},{7,9},{8,6},{9,7},{10,... | collective-permute-start | bytes 147464 | tf_op jit(solution)/shard_map/ppermute | solution.py:624
  26.4 46.2 %collective-permute-start.1 = (bf16[3,32,256]{2,1,0:T(8,128)(2,1)S(1)}, bf16[3,32,256]{2,1,0:T(8,128)(2,1)S(1)}, u32[]{:S(2)}, u32[]{:S(2)}) collective-permute-start(bf16[3,32,256]{2,1,0:T(8,128)(2,1)S(1)} %get-tuple-element.100), channel_id=1, source_target_pairs={{0,1},{1,2},{2,3},{3,0},{4,9},{5,10},{6,11},{7,8},{8,5},{9,6},{10,... | collective-permute-start | bytes 147464 | tf_op jit(solution)/shard_map/ppermute | solution.py:624
  32.3 39.2 %collective-permute-start = (bf16[3,32,256]{2,1,0:T(8,128)(2,1)S(1)}, bf16[3,32,256]{2,1,0:T(8,128)(2,1)S(1)}, u32[]{:S(2)}, u32[]{:S(2)}) collective-permute-start(bf16[3,32,256]{2,1,0:T(8,128)(2,1)S(1)} %get-tuple-element.101), channel_id=1, source_target_pairs={{0,0},{1,1},{2,2},{3,3},{4,8},{5,9},{6,10},{7,11},{8,4},{9,5},{10,... | collective-permute-start | bytes 147464 | tf_op jit(solution)/shard_map/ppermute | solution.py:624
  74.1 54.6 %all-to-all-start.1 = ((bf16[32,264,128]{2,1,0:T(8,128)(2,1)}), bf16[32,264,128]{2,1,0:T(8,128)(2,1)S(1)}, u32[]{:S(2)}, u32[]{:S(2)}) async-start(bf16[32,264,128]{2,1,0:T(8,128)(2,1)} %pack.3), calls=%async_computation.1 | async-start | bytes 4325376 | tf_op jit(solution)/shard_map/all_to_all | solution.py:594
  94.6 17.9 %collective-permute-start.8 = (bf16[768,128]{1,0:T(8,128)(2,1)}, bf16[768,128]{1,0:T(8,128)(2,1)S(1)}, u32[]{:S(2)}, u32[]{:S(2)}) collective-permute-start(bf16[768,128]{1,0:T(8,128)(2,1)} %get-tuple-element.61), channel_id=1, source_target_pairs={{0,136},{8,128},{64,200},{72,192},{128,8},{136,0},{192,72},{200,64... | collective-permute-start | bytes 589832 | tf_op jit(solution)/shard_map/ppermute | solution.py:601
  96.5 16.0 %collective-permute-start.9 = (bf16[768,128]{1,0:T(8,128)(2,1)}, bf16[768,128]{1,0:T(8,128)(2,1)S(1)}, u32[]{:S(2)}, u32[]{:S(2)}) collective-permute-start(bf16[768,128]{1,0:T(8,128)(2,1)} %get-tuple-element.62), channel_id=1, source_target_pairs={{0,192},{8,200},{64,0},{72,8},{128,64},{136,72},{192,128},{200,136... | collective-permute-start | bytes 589832 | tf_op jit(solution)/shard_map/ppermute | solution.py:601
  98.4 15.1 %collective-permute-start.10 = (bf16[768,128]{1,0:T(8,128)(2,1)}, bf16[768,128]{1,0:T(8,128)(2,1)S(1)}, u32[]{:S(2)}, u32[]{:S(2)}) collective-permute-start(bf16[768,128]{1,0:T(8,128)(2,1)} %get-tuple-element.63), channel_id=1, source_target_pairs={{0,200},{8,192},{64,8},{72,0},{128,72},{136,64},{192,136},{200,128... | collective-permute-start | bytes 589832 | tf_op jit(solution)/shard_map/ppermute | solution.py:601
  128.7 48.6 %all-to-all-start.2 = ((bf16[32,48,128]{2,1,0:T(8,128)(2,1)}), bf16[32,48,128]{2,1,0:T(8,128)(2,1)S(1)}, u32[]{:S(2)}, u32[]{:S(2)}) async-start(bf16[32,48,128]{2,1,0:T(8,128)(2,1)} %analyse.2), calls=%async_computation.2 | async-start | bytes 786432 | tf_op jit(solution)/shard_map/all_to_all | solution.py:594
  140.5 20.8 %collective-permute-start.11 = (bf16[3,128,256]{2,1,0:T(8,128)(2,1)S(1)}, bf16[3,128,256]{2,1,0:T(8,128)(2,1)S(1)}, u32[]{:S(2)}, u32[]{:S(2)}) collective-permute-start(bf16[3,128,256]{2,1,0:T(8,128)(2,1)S(1)} %bitcast.37), channel_id=1, source_target_pairs={{0,8},{8,0},{1,9},{9,1},{2,10},{10,2},{3,11},{11,3},{4,12},{12,4},... | collective-permute-start | bytes 589832 | tf_op jit(solution)/shard_map/ppermute | solution.py:612
  144.0 26.3 %collective-permute-start.17 = (bf16[3,128,256]{2,1,0:T(8,128)(2,1)S(1)}, bf16[3,128,256]{2,1,0:T(8,128)(2,1)}, u32[]{:S(2)}, u32[]{:S(2)}) collective-permute-start(bf16[3,128,256]{2,1,0:T(8,128)(2,1)S(1)} %collective-permute-done.16.refs_6_), channel_id=1, source_target_pairs={{0,8},{8,0},{1,9},{9,1},{2,10},{10,2},{3,11},{11,3},{4,12},{12,4},... | collective-permute-start | bytes 589832 | tf_op jit(solution)/shard_map/ppermute | solution.py:612
  148.7 22.1 %collective-permute-start.15 = (bf16[3,128,256]{2,1,0:T(8,128)(2,1)S(1)}, bf16[3,128,256]{2,1,0:T(8,128)(2,1)}, u32[]{:S(2)}, u32[]{:S(2)}) collective-permute-start(bf16[3,128,256]{2,1,0:T(8,128)(2,1)S(1)} %collective-permute-done.14.refs_4_), channel_id=1, source_target_pairs={{0,8},{8,0},{1,9},{9,1},{2,10},{10,2},{3,11},{11,3},{4,12},{12,4},... | collective-permute-start | bytes 589832 | tf_op jit(solution)/shard_map/ppermute | solution.py:612
  151.1 23.4 %collective-permute-start.13 = (bf16[3,128,256]{2,1,0:T(8,128)(2,1)S(1)}, bf16[3,128,256]{2,1,0:T(8,128)(2,1)}, u32[]{:S(2)}, u32[]{:S(2)}) collective-permute-start(bf16[3,128,256]{2,1,0:T(8,128)(2,1)S(1)} %collective-permute-done.12.refs_2_), channel_id=1, source_target_pairs={{0,8},{8,0},{1,9},{9,1},{2,10},{10,2},{3,11},{11,3},{4,12},{12,4},... | collective-permute-start | bytes 589832 | tf_op jit(solution)/shard_map/ppermute | solution.py:612
  161.2 16.1 %collective-permute-start.18 = (bf16[768,128]{1,0:T(8,128)(2,1)}, bf16[768,128]{1,0:T(8,128)(2,1)S(1)}, u32[]{:S(2)}, u32[]{:S(2)}) collective-permute-start(bf16[768,128]{1,0:T(8,128)(2,1)} %get-tuple-element.69), channel_id=1, source_target_pairs={{0,8},{8,0},{64,72},{72,64},{128,136},{136,128},{192,200},{200,192... | collective-permute-start | bytes 589832 | tf_op jit(solution)/shard_map/ppermute | solution.py:601
  161.3 18.2 %collective-permute-start.19 = (bf16[768,128]{1,0:T(8,128)(2,1)}, bf16[768,128]{1,0:T(8,128)(2,1)S(1)}, u32[]{:S(2)}, u32[]{:S(2)}) collective-permute-start(bf16[768,128]{1,0:T(8,128)(2,1)} %get-tuple-element.70), channel_id=1, source_target_pairs={{0,64},{8,72},{64,128},{72,136},{128,192},{136,200},{192,0},{200,8... | collective-permute-start | bytes 589832 | tf_op jit(solution)/shard_map/ppermute | solution.py:601
  170.3 23.1 %collective-permute-start.20 = (bf16[768,128]{1,0:T(8,128)(2,1)}, bf16[768,128]{1,0:T(8,128)(2,1)S(1)}, u32[]{:S(2)}, u32[]{:S(2)}) collective-permute-start(bf16[768,128]{1,0:T(8,128)(2,1)} %get-tuple-element.71), channel_id=1, source_target_pairs={{0,72},{8,64},{64,136},{72,128},{128,200},{136,192},{192,8},{200,0... | collective-permute-start | bytes 589832 | tf_op jit(solution)/shard_map/ppermute | solution.py:601
  170.8 22.6 %collective-permute-start.21 = (bf16[768,128]{1,0:T(8,128)(2,1)}, bf16[768,128]{1,0:T(8,128)(2,1)S(1)}, u32[]{:S(2)}, u32[]{:S(2)}) collective-permute-start(bf16[768,128]{1,0:T(8,128)(2,1)} %get-tuple-element.72), channel_id=1, source_target_pairs={{0,128},{8,136},{64,192},{72,200},{128,0},{136,8},{192,64},{200,72... | collective-permute-start | bytes 589832 | tf_op jit(solution)/shard_map/ppermute | solution.py:601
  174.5 19.0 %collective-permute-start.22 = (bf16[768,128]{1,0:T(8,128)(2,1)}, bf16[768,128]{1,0:T(8,128)(2,1)S(1)}, u32[]{:S(2)}, u32[]{:S(2)}) collective-permute-start(bf16[768,128]{1,0:T(8,128)(2,1)} %get-tuple-element.73), channel_id=1, source_target_pairs={{0,136},{8,128},{64,200},{72,192},{128,8},{136,0},{192,72},{200,64... | collective-permute-start | bytes 589832 | tf_op jit(solution)/shard_map/ppermute | solution.py:601
  177.3 16.2 %collective-permute-start.23 = (bf16[768,128]{1,0:T(8,128)(2,1)S(1)}, bf16[768,128]{1,0:T(8,128)(2,1)S(1)}, u32[]{:S(2)}, u32[]{:S(2)}) collective-permute-start(bf16[768,128]{1,0:T(8,128)(2,1)S(1)} %copy-done.18), channel_id=1, source_target_pairs={{0,192},{8,200},{64,0},{72,8},{128,64},{136,72},{192,128},{200,136... | collective-permute-start | bytes 589832 | tf_op jit(solution)/shard_map/ppermute | solution.py:601
  184.1 24.5 %all-to-all-start.3 = ((bf16[32,48,128]{2,1,0:T(8,128)(2,1)}), bf16[32,48,128]{2,1,0:T(8,128)(2,1)S(1)}, u32[]{:S(2)}, u32[]{:S(2)}) async-start(bf16[32,48,128]{2,1,0:T(8,128)(2,1)} %mix.1), calls=%async_computation.3 | async-start | bytes 786432 | tf_op jit(solution)/shard_map/all_to_all | solution.py:594
  220.4 21.0 %collective-permute-start.27 = (bf16[768,128]{1,0:T(8,128)(2,1)}, bf16[768,128]{1,0:T(8,128)(2,1)S(1)}, u32[]{:S(2)}, u32[]{:S(2)}) collective-permute-start(bf16[768,128]{1,0:T(8,128)(2,1)} %get-tuple-element.80), channel_id=1, source_target_pairs={{0,72},{8,64},{64,136},{72,128},{128,200},{136,192},{192,8},{200,0... | collective-permute-start | bytes 589832 | tf_op jit(solution)/shard_map/ppermute | solution.py:601
  220.4 21.0 %collective-permute-start.28 = (bf16[768,128]{1,0:T(8,128)(2,1)}, bf16[768,128]{1,0:T(8,128)(2,1)S(1)}, u32[]{:S(2)}, u32[]{:S(2)}) collective-permute-start(bf16[768,128]{1,0:T(8,128)(2,1)} %get-tuple-element.81), channel_id=1, source_target_pairs={{0,128},{8,136},{64,192},{72,200},{128,0},{136,8},{192,64},{200,72... | collective-permute-start | bytes 589832 | tf_op jit(solution)/shard_map/ppermute | solution.py:601
  224.5 16.9 %collective-permute-start.29 = (bf16[768,128]{1,0:T(8,128)(2,1)}, bf16[768,128]{1,0:T(8,128)(2,1)S(1)}, u32[]{:S(2)}, u32[]{:S(2)}) collective-permute-start(bf16[768,128]{1,0:T(8,128)(2,1)} %get-tuple-element.82), channel_id=1, source_target_pairs={{0,136},{8,128},{64,200},{72,192},{128,8},{136,0},{192,72},{200,64... | collective-permute-start | bytes 589832 | tf_op jit(solution)/shard_map/ppermute | solution.py:601
  224.6 16.8 %collective-permute-start.30 = (bf16[768,128]{1,0:T(8,128)(2,1)}, bf16[768,128]{1,0:T(8,128)(2,1)S(1)}, u32[]{:S(2)}, u32[]{:S(2)}) collective-permute-start(bf16[768,128]{1,0:T(8,128)(2,1)} %get-tuple-element.83), channel_id=1, source_target_pairs={{0,192},{8,200},{64,0},{72,8},{128,64},{136,72},{192,128},{200,136... | collective-permute-start | bytes 589832 | tf_op jit(solution)/shard_map/ppermute | solution.py:601
  228.9 22.9 %all-to-all-start.5 = ((bf16[32,48,128]{2,1,0:T(8,128)(2,1)}), bf16[32,48,128]{2,1,0:T(8,128)(2,1)S(1)}, u32[]{:S(2)}, u32[]{:S(2)}) async-start(bf16[32,48,128]{2,1,0:T(8,128)(2,1)} %analyse.3), calls=%async_computation.5 | async-start | bytes 786432 | tf_op jit(solution)/shard_map/all_to_all | solution.py:594
  251.7 59.0 %all-to-all-start.4 = ((bf16[32,264,128]{2,1,0:T(8,128)(2,1)}), bf16[32,264,128]{2,1,0:T(8,128)(2,1)S(1)}, u32[]{:S(2)}, u32[]{:S(2)}) async-start(bf16[32,264,128]{2,1,0:T(8,128)(2,1)} %inverse.1), calls=%async_computation.4 | async-start | bytes 4325376 | tf_op jit(solution)/shard_map/all_to_all | solution.py:594
  269.1 20.5 %collective-permute-start.34 = (f32[3,128,256]{2,1,0:T(8,128)}, f32[3,128,256]{2,1,0:T(8,128)S(1)}, u32[]{:S(2)}, u32[]{:S(2)}) collective-permute-start(f32[3,128,256]{2,1,0:T(8,128)} %get-tuple-element.91), channel_id=1, source_target_pairs={{0,128},{64,192},{128,0},{192,64},{1,129},{65,193},{129,1},{193,65... | collective-permute-start | bytes 1179656 | tf_op jit(solution)/shard_map/ppermute | solution.py:607
  272.1 17.5 %collective-permute-start.35 = (f32[3,128,256]{2,1,0:T(8,128)}, f32[3,128,256]{2,1,0:T(8,128)S(1)}, u32[]{:S(2)}, u32[]{:S(2)}) collective-permute-start(f32[3,128,256]{2,1,0:T(8,128)} %get-tuple-element.92), channel_id=1, source_target_pairs={{0,192},{64,0},{128,64},{192,128},{1,193},{65,1},{129,65},{193,129... | collective-permute-start | bytes 1179656 | tf_op jit(solution)/shard_map/ppermute | solution.py:607
  292.7 23.7 %collective-permute-start.36 = (f32[3,32,256]{2,1,0:T(8,128)}, f32[3,32,256]{2,1,0:T(8,128)S(1)}, u32[]{:S(2)}, u32[]{:S(2)}) collective-permute-start(f32[3,32,256]{2,1,0:T(8,128)} %get-tuple-element.93), channel_id=1, source_target_pairs={{0,0},{1,1},{2,2},{3,3},{4,8},{5,9},{6,10},{7,11},{8,4},{9,5},{10,... | collective-permute-start | bytes 294920 | tf_op jit(solution)/shard_map/ppermute | solution.py:624
  301.1 15.3 %collective-permute-start.37 = (f32[3,32,256]{2,1,0:T(8,128)}, f32[3,32,256]{2,1,0:T(8,128)S(1)}, u32[]{:S(2)}, u32[]{:S(2)}) collective-permute-start(f32[3,32,256]{2,1,0:T(8,128)} %get-tuple-element.95), channel_id=1, source_target_pairs={{0,1},{1,2},{2,3},{3,0},{4,9},{5,10},{6,11},{7,8},{8,5},{9,6},{10,... | collective-permute-start | bytes 294920 | tf_op jit(solution)/shard_map/ppermute | solution.py:624
  302.1 15.2 %collective-permute-start.38 = (f32[3,32,256]{2,1,0:T(8,128)}, f32[3,32,256]{2,1,0:T(8,128)S(1)}, u32[]{:S(2)}, u32[]{:S(2)}) collective-permute-start(f32[3,32,256]{2,1,0:T(8,128)} %get-tuple-element.96), channel_id=1, source_target_pairs={{0,2},{1,3},{2,0},{3,1},{4,10},{5,11},{6,8},{7,9},{8,6},{9,7},{10,... | collective-permute-start | bytes 294920 | tf_op jit(solution)/shard_map/ppermute | solution.py:624
  (54 other events, 454.6 us)

commit v2 on v1

--- a/solution.py
+++ b/solution.py
@@ -443,7 +443,7 @@
         jax.ShapeDtypeStruct((8, 3, 128, CH), BF16),
         [position, *pieces],
         specs=[SMEM] + [None] * 8,
-        us=1,
+        us=2,
         name="gather",
     )
 
@@ -689,7 +689,7 @@
     weights = along_x([after(weights, packed_adjoint, sent_x)] * 4)
     weights = [w for near in weights for w in (near, other_core(near))]
     weights = gather(where, weights).reshape(4, 2, 3, 128, CH)
-    pieces_x = fourier(where, sent_x, forward, jnp.broadcast_to(own[None, :], (8, 128)), 1)
+    pieces_x = fourier(where, sent_x, forward, jnp.broadcast_to(own[None, :], (8, 128)), 9)
     mixed = swap(mix(after(adjoint, pieces_x[0]), weights))
     coefficients = analyse(where, cross(pieces_x), table)
     mixed = after(mixed, coefficients)

time: 326 us -> 319 us (0.979)
  starting transfers between devices: 136 us -> 132 us
    ppermute x5, starting transfers between devices: 10.4 us -> 4.42 us  [other_core(): return lax.ppermute(value, 'core', [(0, 1), (1, 0)])]
    unnamed x80 -> x84, local copies, waits for them, and re-layouts: 8.66 us -> 8.48 us
  transfers between devices with their start and end apart: 46 -> 46, of which waited for: 19 -> 16; matrix products, arithmetic and copies ran while one was open for 3% -> 3% of each run, Pallas kernels for 29% -> 30%
where the time goes in v2:
time: 319 us; the launch traced here: 313 us
  starting transfers between devices  132 us (41%)
  Pallas kernels  108 us (34%)
  waiting for transfers between devices  54.1 us (17%)
  local copies, waits for them, and re-layouts  11.8 us (4%)
  other arithmetic  6.02 us (2%)
    pallas_call x16, Pallas kernels, call(): pl.pallas_call(body, out_shape=outs, grid=grid, in_specs=[whole(a) if s i...  108 us
    all_to_all x6, starting transfers between devices, swap(): return lax.all_to_all(value, RING, split_axis=0, concat_axis=0, tiled=True)  46.2 us
    ppermute x21, starting transfers between devices, cross(): moved.append(lax.ppermute(pieces[k], CROSS, pairs))  39.7 us
    ppermute x8, starting transfers between devices, turned(): moved.append(lax.ppermute(piece, ('core', 'zhi', 'y'), pairs))  34.6 us
    ppermute x21, waiting for transfers between devices, cross(): moved.append(lax.ppermute(pieces[k], CROSS, pairs))  22.1 us
    ppermute x6, waiting for transfers between devices, along_x(): lax.ppermute(pieces[dx], 'x', [(i, (i + dx) % 4) for i in range(4)])  17.5 us
    unnamed x84, local copies, waits for them, and re-layouts  8.48 us
    ppermute x6, starting transfers between devices, along_x(): lax.ppermute(pieces[dx], 'x', [(i, (i + dx) % 4) for i in range(4)])  7.4 us
  transfers between devices with their start and end apart: 46, of which 16 were waited for; matrix products, arithmetic and copies ran while one was open for 3% of the time, Pallas kernels for 30%

profile of v2, /device:TPU:1, one launch (start us, length us, event | category | flops | bytes accessed | tf_op | source)
XLA Modules:
  0.0 313.5 jit_solution(15656020451074275884)
XLA Ops:
  0.6 4.7 %pack.2 = bf16[32,264,128]{2,1,0:T(8,128)(2,1)} custom-call(s32[1]{0:T(128)} %bitcast.p_ref, bf16[22,180,256]{2,1,0:T(8,128)(2,1)} %g_ref.1), custom_call_target="tpu_custom_call" | custom-call | flops 5500000256 | bytes 5000000 | tf_op jit(solution)/shard_map/pack/pallas_call | solution.py:25
  5.3 12.2 %all-to-all-start = ((bf16[32,264,128]{2,1,0:T(8,128)(2,1)}), bf16[32,264,128]{2,1,0:T(8,128)(2,1)S(1)}, u32[]{:S(2)}, u32[]{:S(2)}) async-start(bf16[32,264,128]{2,1,0:T(8,128)(2,1)} %pack.2), calls=%async_computation | async-start | bytes 4325376 | tf_op jit(solution)/shard_map/all_to_all | solution.py:594
  17.6 8.4 %collective-permute-start.3 = (bf16[3,32,256]{2,1,0:T(8,128)(2,1)S(1)}, bf16[3,32,256]{2,1,0:T(8,128)(2,1)S(1)}, u32[]{:S(2)}, u32[]{:S(2)}) collective-permute-start(bf16[3,32,256]{2,1,0:T(8,128)(2,1)S(1)} %get-tuple-element.98), channel_id=1, source_target_pairs={{0,3},{1,0},{2,1},{3,2},{4,11},{5,8},{6,9},{7,10},{8,7},{9,4},{10,... | collective-permute-start | bytes 147464 | tf_op jit(solution)/shard_map/ppermute | solution.py:624
  26.4 5.8 %collective-permute-start.1 = (bf16[3,32,256]{2,1,0:T(8,128)(2,1)S(1)}, bf16[3,32,256]{2,1,0:T(8,128)(2,1)S(1)}, u32[]{:S(2)}, u32[]{:S(2)}) collective-permute-start(bf16[3,32,256]{2,1,0:T(8,128)(2,1)S(1)} %get-tuple-element.100), channel_id=1, source_target_pairs={{0,1},{1,2},{2,3},{3,0},{4,9},{5,10},{6,11},{7,8},{8,5},{9,6},{10,... | collective-permute-start | bytes 147464 | tf_op jit(solution)/shard_map/ppermute | solution.py:624
  34.6 4.6 %pack.3 = bf16[32,264,128]{2,1,0:T(8,128)(2,1)} custom-call(s32[1]{0:T(128)} %bitcast.p_ref, bf16[22,180,256]{2,1,0:T(8,128)(2,1)} %x_ref.2), custom_call_target="tpu_custom_call" | custom-call | flops 5500000256 | bytes 5000000 | tf_op jit(solution)/shard_map/pack/pallas_call | solution.py:25
  40.7 4.9 %sine_select_fusion = (f32[768,256]{1,0:T(8,128)}, f32[768,256]{1,0:T(8,128)}) fusion(s32[768]{0:T(1024)S(1)} %get-tuple-element.108, s32[768]{0:T(1024)S(1)} %get-tuple-element.107, s32[256]{0:T(256)S(1)} %compare_select_fusion, pred[256]{0:T(512)(128)(4,1)S(1)} %broadcast_compare_fusion.1), kind=kLoop, calls=%fused_computation.3 | loop fusion | flops 2359296 | bytes 1580288 | tf_op jit(solution)/shard_map/jit(_where)/select_n | solution.py:115
  46.2 19.9 %legendre.1.refs_8_.refs_9_.refs_10_.refs_0_.refs_1_.refs_2_ = bf16[12,8,128,512]{3,2,1,0:T(8,128)(2,1)} custom-call(f32[48,128]{1,0:T(8,128)} %broadcast_in_dim.123.m_ref, f32[8,512]{1,0:T(8,128)} %broadcast_in_dim.125.cos_ref, f32[48,512]{1,0:T(8,128)} %add_select_fusion.1.log_ref), custom_call_target="tpu_custom_call" | custom-call | flops 27499999232 | bytes 25000000 | tf_op jit(solution)/shard_map/legendre/pallas_call | solution.py:25
  66.1 4.5 %waves.1 = (bf16[768,1536]{1,0:T(8,128)(2,1)}, bf16[768,1536]{1,0:T(8,128)(2,1)}) custom-call(f32[768,256]{1,0:T(8,128)} %get-tuple-element.103.c_ref, f32[768,256]{1,0:T(8,128)} %get-tuple-element.102.s_ref), custom_call_target="tpu_custom_call" | custom-call | flops 4400000000 | bytes 4000000 | tf_op jit(solution)/shard_map/waves/pallas_call | solution.py:25
  74.1 6.2 %all-to-all-start.1 = ((bf16[32,264,128]{2,1,0:T(8,128)(2,1)}), bf16[32,264,128]{2,1,0:T(8,128)(2,1)}, u32[]{:S(2)}, u32[]{:S(2)}) async-start(bf16[32,264,128]{2,1,0:T(8,128)(2,1)} %pack.3), calls=%async_computation.1 | async-start | bytes 4325376 | tf_op jit(solution)/shard_map/all_to_all | solution.py:594
  80.9 8.1 %fourier.2 = (bf16[768,128]{1,0:T(8,128)(2,1)}, bf16[768,128]{1,0:T(8,128)(2,1)}, bf16[768,128]{1,0:T(8,128)(2,1)}, bf16[768,128]{1,0:T(8,128)(2,1)}, bf16[768,1...) custom-call(s32[1]{0:T(128)} %bitcast.p_ref, ...), custom_call_target="tpu_custom_call" | custom-call | flops 9900000256 | bytes 9000000 | tf_op jit(solution)/shard_map/fourier/pallas_call | solution.py:25
  103.3 4.8 %collective-permute-done.7.refs_4_ = bf16[768,128]{1,0:T(8,128)(2,1)S(1)} collective-permute-done((bf16[768,128]{1,0:T(8,128)(2,1)}, bf16[768,128]{1,0:T(8,128)(2,1)S(1)}, u32[]{:S(2)}, u32[]{:S(2)}) %collective-permute-start.7) | collective-permute-done | bytes 196640 | tf_op jit(solution)/shard_map/ppermute | solution.py:601
  108.1 4.6 %collective-permute-done.8.refs_5_ = bf16[768,128]{1,0:T(8,128)(2,1)S(1)} collective-permute-done((bf16[768,128]{1,0:T(8,128)(2,1)}, bf16[768,128]{1,0:T(8,128)(2,1)S(1)}, u32[]{:S(2)}, u32[]{:S(2)}) %collective-permute-start.8) | collective-permute-done | bytes 196640 | tf_op jit(solution)/shard_map/ppermute | solution.py:601
  114.5 10.5 %analyse.2 = bf16[32,48,128]{2,1,0:T(8,128)(2,1)} custom-call(s32[1]{0:T(128)} %bitcast.p_ref, bf16[768,128]{1,0:T(8,128)(2,1)} %get-tuple-element.56.refs_0_, bf16[768,128]{1,0:T(8,128)(2,1)} %copy-done.27, bf16[768,128]{1,0:T(8,128)(2,1)} %copy-done.30, bf16[768,128]{1,0:T(8,128)(2,1)} %copy-done.32, bf16[768,128]{1,0:T(8,128)(2,1)} %copy-done.34, ...), custom_call_target="tpu_custom_call" | custom-call | flops 11000000512 | bytes 10000000 | tf_op jit(solution)/shard_map/analyse/pallas_call | solution.py:25
  125.0 3.8 %all-to-all-done.1.r_ref = bf16[32,264,128]{2,1,0:T(8,128)(2,1)} async-done(((bf16[32,264,128]{2,1,0:T(8,128)(2,1)}), bf16[32,264,128]{2,1,0:T(8,128)(2,1)}, u32[]{:S(2)}, u32[]{:S(2)}) %all-to-all-start.1) | async-done | bytes 2162720 | tf_op jit(solution)/shard_map/all_to_all | solution.py:594
  132.5 3.1 collective-permute-start.11
  135.6 7.5 %all-to-all-start.2 = ((bf16[32,48,128]{2,1,0:T(8,128)(2,1)}), bf16[32,48,128]{2,1,0:T(8,128)(2,1)S(1)}, u32[]{:S(2)}, u32[]{:S(2)}) async-start(bf16[32,48,128]{2,1,0:T(8,128)(2,1)} %analyse.2), calls=%async_computation.2 | async-start | bytes 786432 | tf_op jit(solution)/shard_map/all_to_all | solution.py:594
  144.9 8.1 %fourier.3 = (bf16[768,128]{1,0:T(8,128)(2,1)}, bf16[768,128]{1,0:T(8,128)(2,1)}, bf16[768,128]{1,0:T(8,128)(2,1)}, bf16[768,128]{1,0:T(8,128)(2,1)}, bf16[768,1...) custom-call(s32[1]{0:T(128)} %bitcast.p_ref, ...), custom_call_target="tpu_custom_call" | custom-call | flops 9900000256 | bytes 9000000 | tf_op jit(solution)/shard_map/fourier/pallas_call | solution.py:25
  153.2 10.3 %collective-permute-start.19 = (bf16[768,128]{1,0:T(8,128)(2,1)}, bf16[768,128]{1,0:T(8,128)(2,1)S(1)}, u32[]{:S(2)}, u32[]{:S(2)}) collective-permute-start(bf16[768,128]{1,0:T(8,128)(2,1)} %get-tuple-element.70), channel_id=1, source_target_pairs={{0,64},{8,72},{64,128},{72,136},{128,192},{136,200},{192,0},{200,8... | collective-permute-start | bytes 589832 | tf_op jit(solution)/shard_map/ppermute | solution.py:601
  176.1 9.3 %all-to-all-start.3 = ((bf16[32,48,128]{2,1,0:T(8,128)(2,1)}), bf16[32,48,128]{2,1,0:T(8,128)(2,1)S(1)}, u32[]{:S(2)}, u32[]{:S(2)}) async-start(bf16[32,48,128]{2,1,0:T(8,128)(2,1)} %mix.1), calls=%async_computation.3 | async-start | bytes 786432 | tf_op jit(solution)/shard_map/all_to_all | solution.py:594
  186.9 10.5 %analyse.3 = bf16[32,48,128]{2,1,0:T(8,128)(2,1)} custom-call(s32[1]{0:T(128)} %bitcast.p_ref, bf16[768,128]{1,0:T(8,128)(2,1)} %get-tuple-element.66.refs_0_, bf16[768,128]{1,0:T(8,128)(2,1)} %copy-done.16, bf16[768,128]{1,0:T(8,128)(2,1)} %copy-done.18, bf16[768,128]{1,0:T(8,128)(2,1)} %copy-done.20, bf16[768,128]{1,0:T(8,128)(2,1)} %copy-done.21, ...), custom_call_target="tpu_custom_call" | custom-call | flops 11000000512 | bytes 10000000 | tf_op jit(solution)/shard_map/analyse/pallas_call | solution.py:25
  200.7 9.4 %synthesise.1 = (bf16[768,128]{1,0:T(8,128)(2,1)}, bf16[768,128]{1,0:T(8,128)(2,1)}, bf16[768,128]{1,0:T(8,128)(2,1)}, bf16[768,128]{1,0:T(8,128)(2,1)}, bf16[76...) custom-call(s32[1]{0:T(128)} %bitcast.p_ref, ...), custom_call_target="tpu_custom_call" | custom-call | flops 11000000512 | bytes 10000000 | tf_op jit(solution)/shard_map/synthesise/pallas_call | solution.py:25
  221.1 5.9 %all-to-all-start.5 = ((bf16[32,48,128]{2,1,0:T(8,128)(2,1)}), bf16[32,48,128]{2,1,0:T(8,128)(2,1)S(1)}, u32[]{:S(2)}, u32[]{:S(2)}) async-start(bf16[32,48,128]{2,1,0:T(8,128)(2,1)} %analyse.3), calls=%async_computation.5 | async-start | bytes 786432 | tf_op jit(solution)/shard_map/all_to_all | solution.py:594
  227.1 6.3 %collective-permute-done.27.refs_3_ = bf16[768,128]{1,0:T(8,128)(2,1)S(1)} collective-permute-done((bf16[768,128]{1,0:T(8,128)(2,1)}, bf16[768,128]{1,0:T(8,128)(2,1)S(1)}, u32[]{:S(2)}, u32[]{:S(2)}) %collective-permute-start.27) | collective-permute-done | bytes 196640 | tf_op jit(solution)/shard_map/ppermute | solution.py:601
  236.5 8.8 %inverse.1 = bf16[32,264,128]{2,1,0:T(8,128)(2,1)} custom-call(s32[1]{0:T(128)} %bitcast.p_ref, bf16[768,128]{1,0:T(8,128)(2,1)} %get-tuple-element.77.refs_0_, bf16[768,128]{1,0:T(8,128)(2,1)} %copy-done.24, bf16[768,128]{1,0:T(8,128)(2,1)} %copy-done.26, bf16[768,128]{1,0:T(8,128)(2,1)} %copy-done.28, bf16[768,128]{1,0:T(8,128)(2,1)} %copy-done.31, ...), custom_call_target="tpu_custom_call" | custom-call | flops 9900000256 | bytes 9000000 | tf_op jit(solution)/shard_map/inverse/pallas_call | solution.py:25
  245.2 5.1 %all-to-all-start.4 = ((bf16[32,264,128]{2,1,0:T(8,128)(2,1)}), bf16[32,264,128]{2,1,0:T(8,128)(2,1)S(1)}, u32[]{:S(2)}, u32[]{:S(2)}) async-start(bf16[32,264,128]{2,1,0:T(8,128)(2,1)} %inverse.1), calls=%async_computation.4 | async-start | bytes 4325376 | tf_op jit(solution)/shard_map/all_to_all | solution.py:594
  250.4 3.4 %grad.1 = (f32[4,3,128,256]{3,2,1,0:T(8,128)}, f32[4,3,128,256]{3,2,1,0:T(8,128)}) custom-call(s32[1]{0:T(128)} %bitcast.p_ref, bf16[32,48,128]{2,1,0:T(8,128)(2,1)} %copy-done.4, bf16[32,48,128]{2,1,0:T(8,128)(2,1)} %copy-done.2), custom_call_target="tpu_custom_call" | custom-call | flops 4400000000 | bytes 4000000 | tf_op jit(solution)/shard_map/grad/pallas_call | solution.py:25
  253.9 3.5 %collective-permute-done.32.b_ref = f32[4,3,128,256]{3,2,1,0:T(8,128)S(1)} collective-permute-done((f32[4,3,128,256]{3,2,1,0:T(8,128)}, f32[4,3,128,256]{3,2,1,0:T(8,128)S(1)}, u32[]{:S(2)}, u32[]{:S(2)}) %collective-permute-start.32) | collective-permute-done | bytes 1572896 | tf_op jit(solution)/shard_map/ppermute | solution.py:612
  265.5 8.2 %collective-permute-done.33.refs_1_ = f32[3,128,256]{2,1,0:T(8,128)S(1)} collective-permute-done((f32[3,128,256]{2,1,0:T(8,128)}, f32[3,128,256]{2,1,0:T(8,128)S(1)}, u32[]{:S(2)}, u32[]{:S(2)}) %collective-permute-start.33) | collective-permute-done | bytes 393248 | tf_op jit(solution)/shard_map/ppermute | solution.py:607
  273.7 9.3 %collective-permute-done.34.refs_2_ = f32[3,128,256]{2,1,0:T(8,128)S(1)} collective-permute-done((f32[3,128,256]{2,1,0:T(8,128)}, f32[3,128,256]{2,1,0:T(8,128)S(1)}, u32[]{:S(2)}, u32[]{:S(2)}) %collective-permute-start.34) | collective-permute-done | bytes 393248 | tf_op jit(solution)/shard_map/ppermute | solution.py:607
  286.0 8.4 %collective-permute-start.36 = (f32[3,32,256]{2,1,0:T(8,128)}, f32[3,32,256]{2,1,0:T(8,128)S(1)}, u32[]{:S(2)}, u32[]{:S(2)}) collective-permute-start(f32[3,32,256]{2,1,0:T(8,128)} %get-tuple-element.93), channel_id=1, source_target_pairs={{0,0},{1,1},{2,2},{3,3},{4,8},{5,9},{6,10},{7,11},{8,4},{9,5},{10,... | collective-permute-start | bytes 294920 | tf_op jit(solution)/shard_map/ppermute | solution.py:624
  295.4 7.8 %collective-permute-start.38 = (f32[3,32,256]{2,1,0:T(8,128)}, f32[3,32,256]{2,1,0:T(8,128)S(1)}, u32[]{:S(2)}, u32[]{:S(2)}) collective-permute-start(f32[3,32,256]{2,1,0:T(8,128)} %get-tuple-element.96), channel_id=1, source_target_pairs={{0,2},{1,3},{2,0},{3,1},{4,10},{5,11},{6,8},{7,9},{8,6},{9,7},{10,... | collective-permute-start | bytes 294920 | tf_op jit(solution)/shard_map/ppermute | solution.py:624
  305.4 4.3 %finish.1 = bf16[22,180,256]{2,1,0:T(8,128)(2,1)} custom-call(s32[1]{0:T(128)} %bitcast.p_ref, bf16[32,264,128]{2,1,0:T(8,128)(2,1)} %copy-done.1, bf16[22,180,256]{2,1,0:T(8,128)(2,1)} %g_ref.1), custom_call_target="tpu_custom_call" | custom-call | flops 4400000000 | bytes 4000000 | tf_op jit(solution)/shard_map/finish/pallas_call | solution.py:25
  (194 shorter events, 79.7 us)
Async XLA Ops:
  5.3 67.4 %all-to-all-start = ((bf16[32,264,128]{2,1,0:T(8,128)(2,1)}), bf16[32,264,128]{2,1,0:T(8,128)(2,1)S(1)}, u32[]{:S(2)}, u32[]{:S(2)}) async-start(bf16[32,264,128]{2,1,0:T(8,128)(2,1)} %pack.2), calls=%async_computation | async-start | bytes 4325376 | tf_op jit(solution)/shard_map/all_to_all | solution.py:594
  17.6 55.1 %collective-permute-start.3 = (bf16[3,32,256]{2,1,0:T(8,128)(2,1)S(1)}, bf16[3,32,256]{2,1,0:T(8,128)(2,1)S(1)}, u32[]{:S(2)}, u32[]{:S(2)}) collective-permute-start(bf16[3,32,256]{2,1,0:T(8,128)(2,1)S(1)} %get-tuple-element.98), channel_id=1, source_target_pairs={{0,3},{1,0},{2,1},{3,2},{4,11},{5,8},{6,9},{7,10},{8,7},{9,4},{10,... | collective-permute-start | bytes 147464 | tf_op jit(solution)/shard_map/ppermute | solution.py:624
  26.0 46.6 %collective-permute-start.2 = (bf16[3,32,256]{2,1,0:T(8,128)(2,1)S(1)}, bf16[3,32,256]{2,1,0:T(8,128)(2,1)S(1)}, u32[]{:S(2)}, u32[]{:S(2)}) collective-permute-start(bf16[3,32,256]{2,1,0:T(8,128)(2,1)S(1)} %get-tuple-element.99), channel_id=1, source_target_pairs={{0,2},{1,3},{2,0},{3,1},{4,10},{5,11},{6,8},{7,9},{8,6},{9,7},{10,... | collective-permute-start | bytes 147464 | tf_op jit(solution)/shard_map/ppermute | solution.py:624
  26.4 46.2 %collective-permute-start.1 = (bf16[3,32,256]{2,1,0:T(8,128)(2,1)S(1)}, bf16[3,32,256]{2,1,0:T(8,128)(2,1)S(1)}, u32[]{:S(2)}, u32[]{:S(2)}) collective-permute-start(bf16[3,32,256]{2,1,0:T(8,128)(2,1)S(1)} %get-tuple-element.100), channel_id=1, source_target_pairs={{0,1},{1,2},{2,3},{3,0},{4,9},{5,10},{6,11},{7,8},{8,5},{9,6},{10,... | collective-permute-start | bytes 147464 | tf_op jit(solution)/shard_map/ppermute | solution.py:624
  32.3 39.2 %collective-permute-start = (bf16[3,32,256]{2,1,0:T(8,128)(2,1)S(1)}, bf16[3,32,256]{2,1,0:T(8,128)(2,1)S(1)}, u32[]{:S(2)}, u32[]{:S(2)}) collective-permute-start(bf16[3,32,256]{2,1,0:T(8,128)(2,1)S(1)} %get-tuple-element.101), channel_id=1, source_target_pairs={{0,0},{1,1},{2,2},{3,3},{4,8},{5,9},{6,10},{7,11},{8,4},{9,5},{10,... | collective-permute-start | bytes 147464 | tf_op jit(solution)/shard_map/ppermute | solution.py:624
  74.1 54.7 %all-to-all-start.1 = ((bf16[32,264,128]{2,1,0:T(8,128)(2,1)}), bf16[32,264,128]{2,1,0:T(8,128)(2,1)}, u32[]{:S(2)}, u32[]{:S(2)}) async-start(bf16[32,264,128]{2,1,0:T(8,128)(2,1)} %pack.3), calls=%async_computation.1 | async-start | bytes 4325376 | tf_op jit(solution)/shard_map/all_to_all | solution.py:594
  94.7 18.0 %collective-permute-start.8 = (bf16[768,128]{1,0:T(8,128)(2,1)}, bf16[768,128]{1,0:T(8,128)(2,1)S(1)}, u32[]{:S(2)}, u32[]{:S(2)}) collective-permute-start(bf16[768,128]{1,0:T(8,128)(2,1)} %get-tuple-element.61), channel_id=1, source_target_pairs={{0,136},{8,128},{64,200},{72,192},{128,8},{136,0},{192,72},{200,64... | collective-permute-start | bytes 589832 | tf_op jit(solution)/shard_map/ppermute | solution.py:601
  96.6 16.1 %collective-permute-start.9 = (bf16[768,128]{1,0:T(8,128)(2,1)}, bf16[768,128]{1,0:T(8,128)(2,1)S(1)}, u32[]{:S(2)}, u32[]{:S(2)}) collective-permute-start(bf16[768,128]{1,0:T(8,128)(2,1)} %get-tuple-element.62), channel_id=1, source_target_pairs={{0,192},{8,200},{64,0},{72,8},{128,64},{136,72},{192,128},{200,136... | collective-permute-start | bytes 589832 | tf_op jit(solution)/shard_map/ppermute | solution.py:601
  132.5 20.7 %collective-permute-start.11 = (bf16[3,128,256]{2,1,0:T(8,128)(2,1)S(1)}, bf16[3,128,256]{2,1,0:T(8,128)(2,1)S(1)}, u32[]{:S(2)}, u32[]{:S(2)}) collective-permute-start(bf16[3,128,256]{2,1,0:T(8,128)(2,1)S(1)} %bitcast.37), channel_id=1, source_target_pairs={{0,8},{8,0},{1,9},{9,1},{2,10},{10,2},{3,11},{11,3},{4,12},{12,4},... | collective-permute-start | bytes 589832 | tf_op jit(solution)/shard_map/ppermute | solution.py:612
  135.6 34.4 %all-to-all-start.2 = ((bf16[32,48,128]{2,1,0:T(8,128)(2,1)}), bf16[32,48,128]{2,1,0:T(8,128)(2,1)S(1)}, u32[]{:S(2)}, u32[]{:S(2)}) async-start(bf16[32,48,128]{2,1,0:T(8,128)(2,1)} %analyse.2), calls=%async_computation.2 | async-start | bytes 786432 | tf_op jit(solution)/shard_map/all_to_all | solution.py:594
  143.1 20.3 %collective-permute-start.17 = (bf16[3,128,256]{2,1,0:T(8,128)(2,1)S(1)}, bf16[3,128,256]{2,1,0:T(8,128)(2,1)S(1)}, u32[]{:S(2)}, u32[]{:S(2)}) collective-permute-start(bf16[3,128,256]{2,1,0:T(8,128)(2,1)S(1)} %collective-permute-done.16.refs_6_), channel_id=1, source_target_pairs={{0,8},{8,0},{1,9},{9,1},{2,10},{10,2},{3,11},{11,3},{4,12},{12,4},... | collective-permute-start | bytes 589832 | tf_op jit(solution)/shard_map/ppermute | solution.py:612
  143.5 20.1 %collective-permute-start.15 = (bf16[3,128,256]{2,1,0:T(8,128)(2,1)S(1)}, bf16[3,128,256]{2,1,0:T(8,128)(2,1)S(1)}, u32[]{:S(2)}, u32[]{:S(2)}) collective-permute-start(bf16[3,128,256]{2,1,0:T(8,128)(2,1)S(1)} %collective-permute-done.14.refs_4_), channel_id=1, source_target_pairs={{0,8},{8,0},{1,9},{9,1},{2,10},{10,2},{3,11},{11,3},{4,12},{12,4},... | collective-permute-start | bytes 589832 | tf_op jit(solution)/shard_map/ppermute | solution.py:612
  143.7 22.7 %collective-permute-start.13 = (bf16[3,128,256]{2,1,0:T(8,128)(2,1)S(1)}, bf16[3,128,256]{2,1,0:T(8,128)(2,1)S(1)}, u32[]{:S(2)}, u32[]{:S(2)}) collective-permute-start(bf16[3,128,256]{2,1,0:T(8,128)(2,1)S(1)} %collective-permute-done.12.refs_2_), channel_id=1, source_target_pairs={{0,8},{8,0},{1,9},{9,1},{2,10},{10,2},{3,11},{11,3},{4,12},{12,4},... | collective-permute-start | bytes 589832 | tf_op jit(solution)/shard_map/ppermute | solution.py:612
  153.0 17.0 %collective-permute-start.18 = (bf16[768,128]{1,0:T(8,128)(2,1)}, bf16[768,128]{1,0:T(8,128)(2,1)S(1)}, u32[]{:S(2)}, u32[]{:S(2)}) collective-permute-start(bf16[768,128]{1,0:T(8,128)(2,1)} %get-tuple-element.69), channel_id=1, source_target_pairs={{0,8},{8,0},{64,72},{72,64},{128,136},{136,128},{192,200},{200,192... | collective-permute-start | bytes 589832 | tf_op jit(solution)/shard_map/ppermute | solution.py:601
  153.2 19.4 %collective-permute-start.19 = (bf16[768,128]{1,0:T(8,128)(2,1)}, bf16[768,128]{1,0:T(8,128)(2,1)S(1)}, u32[]{:S(2)}, u32[]{:S(2)}) collective-permute-start(bf16[768,128]{1,0:T(8,128)(2,1)} %get-tuple-element.70), channel_id=1, source_target_pairs={{0,64},{8,72},{64,128},{72,136},{128,192},{136,200},{192,0},{200,8... | collective-permute-start | bytes 589832 | tf_op jit(solution)/shard_map/ppermute | solution.py:601
  163.4 21.9 %collective-permute-start.20 = (bf16[768,128]{1,0:T(8,128)(2,1)}, bf16[768,128]{1,0:T(8,128)(2,1)S(1)}, u32[]{:S(2)}, u32[]{:S(2)}) collective-permute-start(bf16[768,128]{1,0:T(8,128)(2,1)} %get-tuple-element.71), channel_id=1, source_target_pairs={{0,72},{8,64},{64,136},{72,128},{128,200},{136,192},{192,8},{200,0... | collective-permute-start | bytes 589832 | tf_op jit(solution)/shard_map/ppermute | solution.py:601
  163.6 21.7 %collective-permute-start.21 = (bf16[768,128]{1,0:T(8,128)(2,1)}, bf16[768,128]{1,0:T(8,128)(2,1)S(1)}, u32[]{:S(2)}, u32[]{:S(2)}) collective-permute-start(bf16[768,128]{1,0:T(8,128)(2,1)} %get-tuple-element.72), channel_id=1, source_target_pairs={{0,128},{8,136},{64,192},{72,200},{128,0},{136,8},{192,64},{200,72... | collective-permute-start | bytes 589832 | tf_op jit(solution)/shard_map/ppermute | solution.py:601
  166.4 19.0 %collective-permute-start.22 = (bf16[768,128]{1,0:T(8,128)(2,1)}, bf16[768,128]{1,0:T(8,128)(2,1)S(1)}, u32[]{:S(2)}, u32[]{:S(2)}) collective-permute-start(bf16[768,128]{1,0:T(8,128)(2,1)} %get-tuple-element.73), channel_id=1, source_target_pairs={{0,136},{8,128},{64,200},{72,192},{128,8},{136,0},{192,72},{200,64... | collective-permute-start | bytes 589832 | tf_op jit(solution)/shard_map/ppermute | solution.py:601
  170.0 15.4 %collective-permute-start.23 = (bf16[768,128]{1,0:T(8,128)(2,1)S(1)}, bf16[768,128]{1,0:T(8,128)(2,1)S(1)}, u32[]{:S(2)}, u32[]{:S(2)}) collective-permute-start(bf16[768,128]{1,0:T(8,128)(2,1)S(1)} %copy-done.17), channel_id=1, source_target_pairs={{0,192},{8,200},{64,0},{72,8},{128,64},{136,72},{192,128},{200,136... | collective-permute-start | bytes 589832 | tf_op jit(solution)/shard_map/ppermute | solution.py:601
  176.1 23.9 %all-to-all-start.3 = ((bf16[32,48,128]{2,1,0:T(8,128)(2,1)}), bf16[32,48,128]{2,1,0:T(8,128)(2,1)S(1)}, u32[]{:S(2)}, u32[]{:S(2)}) async-start(bf16[32,48,128]{2,1,0:T(8,128)(2,1)} %mix.1), calls=%async_computation.3 | async-start | bytes 786432 | tf_op jit(solution)/shard_map/all_to_all | solution.py:594
  213.9 19.5 %collective-permute-start.27 = (bf16[768,128]{1,0:T(8,128)(2,1)}, bf16[768,128]{1,0:T(8,128)(2,1)S(1)}, u32[]{:S(2)}, u32[]{:S(2)}) collective-permute-start(bf16[768,128]{1,0:T(8,128)(2,1)} %get-tuple-element.80), channel_id=1, source_target_pairs={{0,72},{8,64},{64,136},{72,128},{128,200},{136,192},{192,8},{200,0... | collective-permute-start | bytes 589832 | tf_op jit(solution)/shard_map/ppermute | solution.py:601
  213.9 19.4 %collective-permute-start.28 = (bf16[768,128]{1,0:T(8,128)(2,1)}, bf16[768,128]{1,0:T(8,128)(2,1)S(1)}, u32[]{:S(2)}, u32[]{:S(2)}) collective-permute-start(bf16[768,128]{1,0:T(8,128)(2,1)} %get-tuple-element.81), channel_id=1, source_target_pairs={{0,128},{8,136},{64,192},{72,200},{128,0},{136,8},{192,64},{200,72... | collective-permute-start | bytes 589832 | tf_op jit(solution)/shard_map/ppermute | solution.py:601
  216.5 16.9 %collective-permute-start.29 = (bf16[768,128]{1,0:T(8,128)(2,1)}, bf16[768,128]{1,0:T(8,128)(2,1)S(1)}, u32[]{:S(2)}, u32[]{:S(2)}) collective-permute-start(bf16[768,128]{1,0:T(8,128)(2,1)} %get-tuple-element.82), channel_id=1, source_target_pairs={{0,136},{8,128},{64,200},{72,192},{128,8},{136,0},{192,72},{200,64... | collective-permute-start | bytes 589832 | tf_op jit(solution)/shard_map/ppermute | solution.py:601
  217.4 15.9 %collective-permute-start.30 = (bf16[768,128]{1,0:T(8,128)(2,1)}, bf16[768,128]{1,0:T(8,128)(2,1)S(1)}, u32[]{:S(2)}, u32[]{:S(2)}) collective-permute-start(bf16[768,128]{1,0:T(8,128)(2,1)} %get-tuple-element.83), channel_id=1, source_target_pairs={{0,192},{8,200},{64,0},{72,8},{128,64},{136,72},{192,128},{200,136... | collective-permute-start | bytes 589832 | tf_op jit(solution)/shard_map/ppermute | solution.py:601
  220.3 15.4 %collective-permute-start.31 = (bf16[768,128]{1,0:T(8,128)(2,1)}, bf16[768,128]{1,0:T(8,128)(2,1)S(1)}, u32[]{:S(2)}, u32[]{:S(2)}) collective-permute-start(bf16[768,128]{1,0:T(8,128)(2,1)} %get-tuple-element.84), channel_id=1, source_target_pairs={{0,200},{8,192},{64,8},{72,0},{128,72},{136,64},{192,136},{200,128... | collective-permute-start | bytes 589832 | tf_op jit(solution)/shard_map/ppermute | solution.py:601
  221.1 24.1 %all-to-all-start.5 = ((bf16[32,48,128]{2,1,0:T(8,128)(2,1)}), bf16[32,48,128]{2,1,0:T(8,128)(2,1)S(1)}, u32[]{:S(2)}, u32[]{:S(2)}) async-start(bf16[32,48,128]{2,1,0:T(8,128)(2,1)} %analyse.3), calls=%async_computation.5 | async-start | bytes 786432 | tf_op jit(solution)/shard_map/all_to_all | solution.py:594
  245.2 58.9 %all-to-all-start.4 = ((bf16[32,264,128]{2,1,0:T(8,128)(2,1)}), bf16[32,264,128]{2,1,0:T(8,128)(2,1)S(1)}, u32[]{:S(2)}, u32[]{:S(2)}) async-start(bf16[32,264,128]{2,1,0:T(8,128)(2,1)} %inverse.1), calls=%async_computation.4 | async-start | bytes 4325376 | tf_op jit(solution)/shard_map/all_to_all | solution.py:594
  262.6 20.3 %collective-permute-start.34 = (f32[3,128,256]{2,1,0:T(8,128)}, f32[3,128,256]{2,1,0:T(8,128)S(1)}, u32[]{:S(2)}, u32[]{:S(2)}) collective-permute-start(f32[3,128,256]{2,1,0:T(8,128)} %get-tuple-element.91), channel_id=1, source_target_pairs={{0,128},{64,192},{128,0},{192,64},{1,129},{65,193},{129,1},{193,65... | collective-permute-start | bytes 1179656 | tf_op jit(solution)/shard_map/ppermute | solution.py:607
  265.5 17.5 %collective-permute-start.35 = (f32[3,128,256]{2,1,0:T(8,128)}, f32[3,128,256]{2,1,0:T(8,128)S(1)}, u32[]{:S(2)}, u32[]{:S(2)}) collective-permute-start(f32[3,128,256]{2,1,0:T(8,128)} %get-tuple-element.92), channel_id=1, source_target_pairs={{0,192},{64,0},{128,64},{192,128},{1,193},{65,1},{129,65},{193,129... | collective-permute-start | bytes 1179656 | tf_op jit(solution)/shard_map/ppermute | solution.py:607
  286.0 23.7 %collective-permute-start.36 = (f32[3,32,256]{2,1,0:T(8,128)}, f32[3,32,256]{2,1,0:T(8,128)S(1)}, u32[]{:S(2)}, u32[]{:S(2)}) collective-permute-start(f32[3,32,256]{2,1,0:T(8,128)} %get-tuple-element.93), channel_id=1, source_target_pairs={{0,0},{1,1},{2,2},{3,3},{4,8},{5,9},{6,10},{7,11},{8,4},{9,5},{10,... | collective-permute-start | bytes 294920 | tf_op jit(solution)/shard_map/ppermute | solution.py:624
  294.4 15.3 %collective-permute-start.37 = (f32[3,32,256]{2,1,0:T(8,128)}, f32[3,32,256]{2,1,0:T(8,128)S(1)}, u32[]{:S(2)}, u32[]{:S(2)}) collective-permute-start(f32[3,32,256]{2,1,0:T(8,128)} %get-tuple-element.95), channel_id=1, source_target_pairs={{0,1},{1,2},{2,3},{3,0},{4,9},{5,10},{6,11},{7,8},{8,5},{9,6},{10,... | collective-permute-start | bytes 294920 | tf_op jit(solution)/shard_map/ppermute | solution.py:624
  295.4 15.2 %collective-permute-start.38 = (f32[3,32,256]{2,1,0:T(8,128)}, f32[3,32,256]{2,1,0:T(8,128)S(1)}, u32[]{:S(2)}, u32[]{:S(2)}) collective-permute-start(f32[3,32,256]{2,1,0:T(8,128)} %get-tuple-element.96), channel_id=1, source_target_pairs={{0,2},{1,3},{2,0},{3,1},{4,10},{5,11},{6,8},{7,9},{8,6},{9,7},{10,... | collective-permute-start | bytes 294920 | tf_op jit(solution)/shard_map/ppermute | solution.py:624
  (56 other events, 414.8 us)
